TPU v7x, 32 devices: a whole 2x2x4 slice. The times are simulated.
32 devices in a mesh: groups: 2 (over x), docs: 8 (over z, y), mods: 2 (over core).
Axes of the slice: x: 2, y: 2, z: 4, core: 2. Of those that a mesh axis runs over, the one named last changes fastest.
Arguments:
- doc_grads: bfloat16 [16384, 24576], P(('groups', 'docs'), 'mods'), parts along dimension 0, may hold values from -6 to 6
- query_grads: bfloat16 [512, 24576], P(('groups', 'docs'), 'mods'), parts along dimension 0, may hold values from -6 to 6
- basis_in: float32 [6, 64, 64], P('mods'), may hold values from -0.75 to 0.75
- basis_out: float32 [6, 64, 64], P('mods'), may hold values from -0.75 to 0.75
- eigen: float32 [6, 64, 64], P('mods'), may hold values from 0.05 to 20
- token_counts: int32 [16384], P(('groups', 'docs')), parts along dimension 0, may hold values from 512 to 2048
Outputs:
- influence: float32 [16384, 256], P(('groups', 'docs')), parts along dimension 0
There are 2 independent parts, one for each index of `groups`. A program takes and returns all parts, laid end to end along the dimension named above; an argument that names none is the same for every part. Nothing has to cross between parts.
All inputs are finite; a program needn't handle non-finite values.
Results may differ from a plain program's by a relative error of at most 0.008.
Values may be sent and summed in bfloat16 or wider, within the bound.
A program may use at most 128 MiB of HBM per device.

v0:
```python
import jax
import jax.numpy as jnp
from jax import lax
from jax.sharding import PartitionSpec as P

ref_tokens = 1024.0


def from_behind(array, axis, by):
    devices = lax.axis_size(axis)
    return lax.ppermute(array, axis, [(i, (i + by) % devices) for i in range(devices)])


def precondition(gradient, basis_in, basis_out, eigen):
    high = lax.Precision.HIGHEST
    rotated = jnp.einsum("qmab,mai->qmib", gradient, basis_in, precision=high)
    rotated = jnp.einsum("qmib,mbj->qmij", rotated, basis_out, precision=high)
    damping = 0.1 * jnp.mean(eigen, axis=(1, 2))
    scaled = rotated / (eigen + damping[:, None, None])
    mapped = jnp.einsum("qmij,mbj->qmib", scaled, basis_out, precision=high)
    mapped = jnp.einsum("qmib,mai->qmab", mapped, basis_in, precision=high)
    self_score = jnp.sum(gradient * mapped, axis=(1, 2, 3))
    return (mapped, self_score)


def shards(doc_grads, query_grads, basis_in, basis_out, eigen, token_counts):
    queries_here = query_grads.shape[0]
    mods_here = basis_in.shape[0]
    module_width = basis_in.shape[1]
    gradient = query_grads.reshape(queries_here, mods_here, module_width, module_width).astype(
        jnp.float32
    )
    mapped, self_part = precondition(gradient, basis_in, basis_out, eigen)
    precond_block = mapped.reshape(queries_here, -1).astype(jnp.bfloat16)
    self_piece = lax.psum(self_part, "mods")
    cycle_size = lax.axis_size("docs")
    position = lax.axis_index("docs")
    total_queries = queries_here * cycle_size

    def record(scores, self_terms, arrived, arrived_self, source):
        partial_value = lax.dot_general(
            doc_grads, arrived, (((1,), (1,)), ((), ())), preferred_element_type=jnp.float32
        )
        column = source * queries_here
        scores = lax.dynamic_update_slice(scores, partial_value, (jnp.int32(0), column))
        self_terms = lax.dynamic_update_slice(self_terms, arrived_self, (column,))
        return (scores, self_terms)

    scores = jnp.zeros((doc_grads.shape[0], total_queries), jnp.float32)
    self_terms = jnp.zeros((total_queries,), jnp.float32)
    scores, self_terms = record(scores, self_terms, precond_block, self_piece, position)

    def advance(offset, carried):
        arrived, arrived_self, scores, self_terms = carried
        arrived, arrived_self = (
            from_behind(arrived, "docs", 1),
            from_behind(arrived_self.astype(jnp.bfloat16), "docs", 1).astype(arrived_self.dtype),
        )
        scores, self_terms = record(
            scores, self_terms, arrived, arrived_self, (position - offset) % cycle_size
        )
        return (arrived, arrived_self, scores, self_terms)

    carried = lax.fori_loop(1, cycle_size, advance, (precond_block, self_piece, scores, self_terms))
    scores, self_terms = (carried[2], carried[3])
    totals = lax.psum(scores.astype(jnp.bfloat16), "mods").astype(jnp.float32)
    factor = ref_tokens / token_counts.astype(jnp.float32)
    return totals / jnp.sqrt(self_terms)[None, :] * factor[:, None]


def solution(mesh):
    in_specs = (
        P(("groups", "docs"), "mods"),
        P(("groups", "docs"), "mods"),
        P("mods", None, None),
        P("mods", None, None),
        P("mods", None, None),
        P(("groups", "docs")),
    )
    out_specs = P(("groups", "docs"), None)
    return jax.shard_map(shards, mesh=mesh, in_specs=in_specs, out_specs=out_specs, check_vma=False)
```

profile of v0, /device:TPU:0, one launch (start us, length us, event | category | flops | bytes accessed | tf_op | source)
XLA Modules:
  0.0 305.3 jit_solution(5790757208798477841)
XLA Ops:
  6.5 2.6 reshape.11
  9.1 0.9 copy.9
  10.0 0.0 copy-start.3
  10.0 0.1 reduce_sum.18
  10.1 0.1 broadcast_add_fusion
  10.2 4.6 %fusion.13 = f32[3,64,32,64]{3,1,2,0:T(8,128)S(1)} fusion(bf16[32,3,64,64]{2,3,0,1:T(8,128)(2,1)S(1)} %copy.9, f32[3,64,64]{2,1,0:T(8,128)S(1)} %copy-done), kind=kOutput, calls=%fused_computation.18 | convolution fusion | flops 301989888 | bytes 2408448 | tf_op jit(solution)/shard_map/qmab,mai->qmib/dot_general | solution.py:16
  14.9 3.0 fusion.5
  17.9 9.1 %fusion.3 = f32[3,32,64,64]{2,3,1,0:T(8,128)S(1)} fusion(f32[3,32,64,64]{3,2,1,0:T(8,128)S(1)} %fusion.5, f32[3,64,64]{2,1,0:T(8,128)S(1)} %broadcast_add_fusion, f32[3,64,64]{2,1,0:T(8,128)S(1)} %copy-done.3), kind=kOutput, calls=%fused_computation.6 | convolution fusion | flops 302383104 | bytes 3244032 | tf_op jit(solution)/shard_map/qmij,mbj->qmib/dot_general | solution.py:20
  27.0 4.5 %bitcast_convert_fusion = (bf16[32,3,64,64]{2,3,0,1:T(8,128)(2,1)}, f32[3,32,64,64]{3,2,1,0:T(8,128)}) fusion(f32[3,64,64]{2,1,0:T(8,128)S(1)} %copy-done, f32[3,32,64,64]{2,3,1,0:T(8,128)S(1)} %fusion.3), kind=kOutput, calls=%fused_computation.2 | convolution fusion | flops 302383104 | bytes 3981312 | tf_op jit(solution)/shard_map/qmib,mai->qmab/dot_general | solution.py:21
  31.5 1.9 copy.8
  33.4 2.0 convert_element_type.39
  35.5 2.6 fusion
  38.1 2.6 psum.14
  40.7 0.2 dynamic_update_slice.27
  40.9 12.2 %fusion.9 = bf16[1024,256]{0,1:T(8,128)(2,1)S(1)} fusion(bf16[1024,256]{0,1:T(8,128)(2,1)S(1)} %broadcast_in_dim.4, s32[]{:T(128)S(6)} %select_n.35, bf16[32,12288]{1,0:T(8,128)(2,1)S(1)} %copy-done.1, bf16[1024,12288]{1,0:T(8,128)(2,1)} %param.8), kind=kOutput, calls=%fused_computation.13 | convolution fusion | flops 805306368 | bytes 26083332 | tf_op jit(solution)/shard_map/dot_general | solution.py:41
  53.2 0.0 copy-start.4
  53.2 227.2 %while.21 = (s32[]{:T(128)}, bf16[32,12288]{1,0:T(8,128)(2,1)S(1)}, f32[32]{0:T(128)S(1)}, bf16[1024,256]{0,1:T(8,128)(2,1)S(1)}, f32[256]{0:T(256)S(1)}, /*inde...) while((s32[]{:T(128)}, bf16[32,12288]{1,0:T(8,128)(2,1)S(1)}, ...), condition=%wide.region_4.5_spmd, body=%wide.region_3.4_spmd.sunk | while | flops 805306432 | bytes 30804284 | solution.py:64
  53.2 2.9 collective-permute-start
  56.1 1.5 collective-permute-start.1
  57.6 19.5 %collective-permute-done.1 = bf16[32]{0:T(256)(128)(2,1)S(1)} collective-permute-done((bf16[32]{0:T(256)(128)(2,1)S(1)}, bf16[32]{0:T(256)(128)(2,1)S(1)}, u32[]{:S(2)}, u32[]{:S(2)}) %collective-permute-start.1) | collective-permute-done | bytes 96 | tf_op jit(solution)/shard_map/while/body/eval_jaxpr/ppermute | solution.py:11
  77.1 0.1 fusion.26
  77.2 0.0 collective-permute-done
  77.2 0.1 copy.32
  77.2 12.2 %convolution_dynamic-update-slice_fusion.2 = bf16[1024,256]{0,1:T(8,128)(2,1)S(1)} fusion(bf16[1024,256]{0,1:T(8,128)(2,1)S(1)} %get-tuple-element.266, s32[]{:T(128)S(6)} %select_n.39, bf16[1024,12288]{1,0:T(8,128)(2,1)} %get-tuple-element.281, bf16[32,12288]{1,0:T(8,128)(2,1)S(1)} %collective-permute-done), kind=kOutput, calls=%fused_computation.clone.1 | convolution fusion | flops 805306368 | bytes 26083332 | tf_op jit(solution)/shard_map/while/body/eval_jaxpr/dot_general | solution.py:41
  89.5 0.1 collective-permute-start
  89.6 1.1 collective-permute-start.1
  90.7 20.7 %collective-permute-done.1 = bf16[32]{0:T(256)(128)(2,1)S(1)} collective-permute-done((bf16[32]{0:T(256)(128)(2,1)S(1)}, bf16[32]{0:T(256)(128)(2,1)S(1)}, u32[]{:S(2)}, u32[]{:S(2)}) %collective-permute-start.1) | collective-permute-done | bytes 96 | tf_op jit(solution)/shard_map/while/body/eval_jaxpr/ppermute | solution.py:11
  111.3 0.1 fusion.26
  111.4 0.1 copy.32
  111.5 12.2 %convolution_dynamic-update-slice_fusion.2 = bf16[1024,256]{0,1:T(8,128)(2,1)S(1)} fusion(bf16[1024,256]{0,1:T(8,128)(2,1)S(1)} %get-tuple-element.266, s32[]{:T(128)S(6)} %select_n.39, bf16[1024,12288]{1,0:T(8,128)(2,1)} %get-tuple-element.281, bf16[32,12288]{1,0:T(8,128)(2,1)S(1)} %collective-permute-done), kind=kOutput, calls=%fused_computation.clone.1 | convolution fusion | flops 805306368 | bytes 26083332 | tf_op jit(solution)/shard_map/while/body/eval_jaxpr/dot_general | solution.py:41
  123.7 0.1 collective-permute-start
  123.8 0.1 collective-permute-start.1
  123.9 20.7 %collective-permute-done.1 = bf16[32]{0:T(256)(128)(2,1)S(1)} collective-permute-done((bf16[32]{0:T(256)(128)(2,1)S(1)}, bf16[32]{0:T(256)(128)(2,1)S(1)}, u32[]{:S(2)}, u32[]{:S(2)}) %collective-permute-start.1) | collective-permute-done | bytes 96 | tf_op jit(solution)/shard_map/while/body/eval_jaxpr/ppermute | solution.py:11
  144.6 0.1 fusion.26
  144.7 0.1 copy.32
  144.8 12.2 %convolution_dynamic-update-slice_fusion.2 = bf16[1024,256]{0,1:T(8,128)(2,1)S(1)} fusion(bf16[1024,256]{0,1:T(8,128)(2,1)S(1)} %get-tuple-element.266, s32[]{:T(128)S(6)} %select_n.39, bf16[1024,12288]{1,0:T(8,128)(2,1)} %get-tuple-element.281, bf16[32,12288]{1,0:T(8,128)(2,1)S(1)} %collective-permute-done), kind=kOutput, calls=%fused_computation.clone.1 | convolution fusion | flops 805306368 | bytes 26083332 | tf_op jit(solution)/shard_map/while/body/eval_jaxpr/dot_general | solution.py:41
  157.0 0.1 collective-permute-start
  157.1 0.1 collective-permute-start.1
  157.2 19.7 %collective-permute-done.1 = bf16[32]{0:T(256)(128)(2,1)S(1)} collective-permute-done((bf16[32]{0:T(256)(128)(2,1)S(1)}, bf16[32]{0:T(256)(128)(2,1)S(1)}, u32[]{:S(2)}, u32[]{:S(2)}) %collective-permute-start.1) | collective-permute-done | bytes 96 | tf_op jit(solution)/shard_map/while/body/eval_jaxpr/ppermute | solution.py:11
  176.9 0.1 fusion.26
  177.0 0.1 copy.32
  177.1 12.2 %convolution_dynamic-update-slice_fusion.2 = bf16[1024,256]{0,1:T(8,128)(2,1)S(1)} fusion(bf16[1024,256]{0,1:T(8,128)(2,1)S(1)} %get-tuple-element.266, s32[]{:T(128)S(6)} %select_n.39, bf16[1024,12288]{1,0:T(8,128)(2,1)} %get-tuple-element.281, bf16[32,12288]{1,0:T(8,128)(2,1)S(1)} %collective-permute-done), kind=kOutput, calls=%fused_computation.clone.1 | convolution fusion | flops 805306368 | bytes 26083332 | tf_op jit(solution)/shard_map/while/body/eval_jaxpr/dot_general | solution.py:41
  189.4 0.1 collective-permute-start
  189.4 0.1 collective-permute-start.1
  189.5 18.7 %collective-permute-done.1 = bf16[32]{0:T(256)(128)(2,1)S(1)} collective-permute-done((bf16[32]{0:T(256)(128)(2,1)S(1)}, bf16[32]{0:T(256)(128)(2,1)S(1)}, u32[]{:S(2)}, u32[]{:S(2)}) %collective-permute-start.1) | collective-permute-done | bytes 96 | tf_op jit(solution)/shard_map/while/body/eval_jaxpr/ppermute | solution.py:11
  208.3 0.1 fusion.26
  208.4 0.1 copy.32
  208.4 12.2 %convolution_dynamic-update-slice_fusion.2 = bf16[1024,256]{0,1:T(8,128)(2,1)S(1)} fusion(bf16[1024,256]{0,1:T(8,128)(2,1)S(1)} %get-tuple-element.266, s32[]{:T(128)S(6)} %select_n.39, bf16[1024,12288]{1,0:T(8,128)(2,1)} %get-tuple-element.281, bf16[32,12288]{1,0:T(8,128)(2,1)S(1)} %collective-permute-done), kind=kOutput, calls=%fused_computation.clone.1 | convolution fusion | flops 805306368 | bytes 26083332 | tf_op jit(solution)/shard_map/while/body/eval_jaxpr/dot_general | solution.py:41
  220.7 0.1 collective-permute-start
  220.8 0.1 collective-permute-start.1
  220.9 17.8 %collective-permute-done.1 = bf16[32]{0:T(256)(128)(2,1)S(1)} collective-permute-done((bf16[32]{0:T(256)(128)(2,1)S(1)}, bf16[32]{0:T(256)(128)(2,1)S(1)}, u32[]{:S(2)}, u32[]{:S(2)}) %collective-permute-start.1) | collective-permute-done | bytes 96 | tf_op jit(solution)/shard_map/while/body/eval_jaxpr/ppermute | solution.py:11
  238.6 0.1 fusion.26
  238.7 0.1 copy.32
  238.8 12.2 %convolution_dynamic-update-slice_fusion.2 = bf16[1024,256]{0,1:T(8,128)(2,1)S(1)} fusion(bf16[1024,256]{0,1:T(8,128)(2,1)S(1)} %get-tuple-element.266, s32[]{:T(128)S(6)} %select_n.39, bf16[1024,12288]{1,0:T(8,128)(2,1)} %get-tuple-element.281, bf16[32,12288]{1,0:T(8,128)(2,1)S(1)} %collective-permute-done), kind=kOutput, calls=%fused_computation.clone.1 | convolution fusion | flops 805306368 | bytes 26083332 | tf_op jit(solution)/shard_map/while/body/eval_jaxpr/dot_general | solution.py:41
  251.0 0.1 collective-permute-start
  251.1 0.1 collective-permute-start.1
  251.2 16.8 %collective-permute-done.1 = bf16[32]{0:T(256)(128)(2,1)S(1)} collective-permute-done((bf16[32]{0:T(256)(128)(2,1)S(1)}, bf16[32]{0:T(256)(128)(2,1)S(1)}, u32[]{:S(2)}, u32[]{:S(2)}) %collective-permute-start.1) | collective-permute-done | bytes 96 | tf_op jit(solution)/shard_map/while/body/eval_jaxpr/ppermute | solution.py:11
  268.0 0.1 fusion.26
  268.1 0.1 copy.32
  268.1 12.2 %convolution_dynamic-update-slice_fusion.2 = bf16[1024,256]{0,1:T(8,128)(2,1)S(1)} fusion(bf16[1024,256]{0,1:T(8,128)(2,1)S(1)} %get-tuple-element.266, s32[]{:T(128)S(6)} %select_n.39, bf16[1024,12288]{1,0:T(8,128)(2,1)} %get-tuple-element.281, bf16[32,12288]{1,0:T(8,128)(2,1)S(1)} %collective-permute-done), kind=kOutput, calls=%fused_computation.clone.1 | convolution fusion | flops 805306368 | bytes 26083332 | tf_op jit(solution)/shard_map/while/body/eval_jaxpr/dot_general | solution.py:41
  280.4 1.0 copy.10
  281.4 0.0 all-reduce.2.cloned.1.call-update
  281.4 14.8 %all-reduce.2.cloned.1.call-done = bf16[1024,256]{1,0:T(8,128)(2,1)} async-done(((bf16[1024,256]{1,0:T(8,128)(2,1)}), bf16[1024,256]{1,0:T(8,128)(2,1)}) %all-reduce.2.cloned.1.call-update) | async-done | bytes 524304 | tf_op jit(solution)/shard_map/psum | solution.py:66
  296.3 2.2 divide_multiply_fusion
  (27 shorter events, 0.1 us)
Async XLA Ops:
  6.5 3.7 %copy-start = (f32[3,64,64]{2,1,0:T(8,128)S(1)}, f32[3,64,64]{2,1,0:T(8,128)}, u32[]{:S(2)}) copy-start(f32[3,64,64]{2,1,0:T(8,128)} %param.10) | copy-start | bytes 147460
  6.5 3.5 %copy-start.2 = (f32[3,64,64]{2,1,0:T(8,128)S(1)}, f32[3,64,64]{2,1,0:T(8,128)}, u32[]{:S(2)}) copy-start(f32[3,64,64]{2,1,0:T(8,128)} %param.12) | copy-start | bytes 147460
  6.5 289.7 %all-reduce.2.cloned.1.call-start = ((), (), s32[]{:S(2)}) async-start(), calls=%async_computation | async-start | bytes 1048576 | tf_op jit(solution)/shard_map/psum | solution.py:66
  10.0 4.9 %copy-start.3 = (f32[3,64,64]{2,1,0:T(8,128)S(1)}, f32[3,64,64]{2,1,0:T(8,128)}, u32[]{:S(2)}) copy-start(f32[3,64,64]{2,1,0:T(8,128)} %param.11) | copy-start | bytes 147460
  35.5 5.4 %copy-start.1 = (bf16[32,12288]{1,0:T(8,128)(2,1)S(1)}, bf16[32,12288]{1,0:T(8,128)(2,1)}, u32[]{:S(2)}) copy-start(bf16[32,12288]{1,0:T(8,128)(2,1)} %convert_element_type.39) | copy-start | bytes 2359300
  53.2 228.2 %copy-start.4 = (s32[1024]{0:T(1024)S(1)}, s32[1024]{0:T(1024)}, u32[]{:S(2)}) copy-start(s32[1024]{0:T(1024)} %param.13) | copy-start | bytes 12292
  53.2 24.0 %collective-permute-start = (bf16[32,12288]{1,0:T(8,128)(2,1)S(1)}, bf16[32,12288]{1,0:T(8,128)(2,1)S(1)}, u32[]{:S(2)}, u32[]{:S(2)}) collective-permute-start(bf16[32,12288]{1,0:T(8,128)(2,1)S(1)} %get-tuple-element.264), channel_id=1, source_target_pairs={{0,2},{2,4},{4,6},{6,8},{8,10},{10,12},{12,14},{14,0},{1,3},{3,5},... | collective-permute-start | bytes 2359304 | tf_op jit(solution)/shard_map/while/body/eval_jaxpr/ppermute | solution.py:11
  56.1 21.0 %collective-permute-start.1 = (bf16[32]{0:T(256)(128)(2,1)S(1)}, bf16[32]{0:T(256)(128)(2,1)S(1)}, u32[]{:S(2)}, u32[]{:S(2)}) collective-permute-start(bf16[32]{0:T(256)(128)(2,1)S(1)} %convert_element_type.52), channel_id=1, source_target_pairs={{0,2},{2,4},{4,6},{6,8},{8,10},{10,12},{12,14},{14,0},{1,3},{3,5},... | collective-permute-start | bytes 200 | tf_op jit(solution)/shard_map/while/body/eval_jaxpr/ppermute | solution.py:11
  89.5 21.9 %collective-permute-start = (bf16[32,12288]{1,0:T(8,128)(2,1)S(1)}, bf16[32,12288]{1,0:T(8,128)(2,1)S(1)}, u32[]{:S(2)}, u32[]{:S(2)}) collective-permute-start(bf16[32,12288]{1,0:T(8,128)(2,1)S(1)} %get-tuple-element.264), channel_id=1, source_target_pairs={{0,2},{2,4},{4,6},{6,8},{8,10},{10,12},{12,14},{14,0},{1,3},{3,5},... | collective-permute-start | bytes 2359304 | tf_op jit(solution)/shard_map/while/body/eval_jaxpr/ppermute | solution.py:11
  89.6 21.8 %collective-permute-start.1 = (bf16[32]{0:T(256)(128)(2,1)S(1)}, bf16[32]{0:T(256)(128)(2,1)S(1)}, u32[]{:S(2)}, u32[]{:S(2)}) collective-permute-start(bf16[32]{0:T(256)(128)(2,1)S(1)} %convert_element_type.52), channel_id=1, source_target_pairs={{0,2},{2,4},{4,6},{6,8},{8,10},{10,12},{12,14},{14,0},{1,3},{3,5},... | collective-permute-start | bytes 200 | tf_op jit(solution)/shard_map/while/body/eval_jaxpr/ppermute | solution.py:11
  123.7 21.0 %collective-permute-start = (bf16[32,12288]{1,0:T(8,128)(2,1)S(1)}, bf16[32,12288]{1,0:T(8,128)(2,1)S(1)}, u32[]{:S(2)}, u32[]{:S(2)}) collective-permute-start(bf16[32,12288]{1,0:T(8,128)(2,1)S(1)} %get-tuple-element.264), channel_id=1, source_target_pairs={{0,2},{2,4},{4,6},{6,8},{8,10},{10,12},{12,14},{14,0},{1,3},{3,5},... | collective-permute-start | bytes 2359304 | tf_op jit(solution)/shard_map/while/body/eval_jaxpr/ppermute | solution.py:11
  123.8 20.8 %collective-permute-start.1 = (bf16[32]{0:T(256)(128)(2,1)S(1)}, bf16[32]{0:T(256)(128)(2,1)S(1)}, u32[]{:S(2)}, u32[]{:S(2)}) collective-permute-start(bf16[32]{0:T(256)(128)(2,1)S(1)} %convert_element_type.52), channel_id=1, source_target_pairs={{0,2},{2,4},{4,6},{6,8},{8,10},{10,12},{12,14},{14,0},{1,3},{3,5},... | collective-permute-start | bytes 200 | tf_op jit(solution)/shard_map/while/body/eval_jaxpr/ppermute | solution.py:11
  157.0 20.0 %collective-permute-start = (bf16[32,12288]{1,0:T(8,128)(2,1)S(1)}, bf16[32,12288]{1,0:T(8,128)(2,1)S(1)}, u32[]{:S(2)}, u32[]{:S(2)}) collective-permute-start(bf16[32,12288]{1,0:T(8,128)(2,1)S(1)} %get-tuple-element.264), channel_id=1, source_target_pairs={{0,2},{2,4},{4,6},{6,8},{8,10},{10,12},{12,14},{14,0},{1,3},{3,5},... | collective-permute-start | bytes 2359304 | tf_op jit(solution)/shard_map/while/body/eval_jaxpr/ppermute | solution.py:11
  157.1 19.8 %collective-permute-start.1 = (bf16[32]{0:T(256)(128)(2,1)S(1)}, bf16[32]{0:T(256)(128)(2,1)S(1)}, u32[]{:S(2)}, u32[]{:S(2)}) collective-permute-start(bf16[32]{0:T(256)(128)(2,1)S(1)} %convert_element_type.52), channel_id=1, source_target_pairs={{0,2},{2,4},{4,6},{6,8},{8,10},{10,12},{12,14},{14,0},{1,3},{3,5},... | collective-permute-start | bytes 200 | tf_op jit(solution)/shard_map/while/body/eval_jaxpr/ppermute | solution.py:11
  189.4 19.0 %collective-permute-start = (bf16[32,12288]{1,0:T(8,128)(2,1)S(1)}, bf16[32,12288]{1,0:T(8,128)(2,1)S(1)}, u32[]{:S(2)}, u32[]{:S(2)}) collective-permute-start(bf16[32,12288]{1,0:T(8,128)(2,1)S(1)} %get-tuple-element.264), channel_id=1, source_target_pairs={{0,2},{2,4},{4,6},{6,8},{8,10},{10,12},{12,14},{14,0},{1,3},{3,5},... | collective-permute-start | bytes 2359304 | tf_op jit(solution)/shard_map/while/body/eval_jaxpr/ppermute | solution.py:11
  189.4 18.8 %collective-permute-start.1 = (bf16[32]{0:T(256)(128)(2,1)S(1)}, bf16[32]{0:T(256)(128)(2,1)S(1)}, u32[]{:S(2)}, u32[]{:S(2)}) collective-permute-start(bf16[32]{0:T(256)(128)(2,1)S(1)} %convert_element_type.52), channel_id=1, source_target_pairs={{0,2},{2,4},{4,6},{6,8},{8,10},{10,12},{12,14},{14,0},{1,3},{3,5},... | collective-permute-start | bytes 200 | tf_op jit(solution)/shard_map/while/body/eval_jaxpr/ppermute | solution.py:11
  220.7 18.0 %collective-permute-start = (bf16[32,12288]{1,0:T(8,128)(2,1)S(1)}, bf16[32,12288]{1,0:T(8,128)(2,1)S(1)}, u32[]{:S(2)}, u32[]{:S(2)}) collective-permute-start(bf16[32,12288]{1,0:T(8,128)(2,1)S(1)} %get-tuple-element.264), channel_id=1, source_target_pairs={{0,2},{2,4},{4,6},{6,8},{8,10},{10,12},{12,14},{14,0},{1,3},{3,5},... | collective-permute-start | bytes 2359304 | tf_op jit(solution)/shard_map/while/body/eval_jaxpr/ppermute | solution.py:11
  220.8 17.9 %collective-permute-start.1 = (bf16[32]{0:T(256)(128)(2,1)S(1)}, bf16[32]{0:T(256)(128)(2,1)S(1)}, u32[]{:S(2)}, u32[]{:S(2)}) collective-permute-start(bf16[32]{0:T(256)(128)(2,1)S(1)} %convert_element_type.52), channel_id=1, source_target_pairs={{0,2},{2,4},{4,6},{6,8},{8,10},{10,12},{12,14},{14,0},{1,3},{3,5},... | collective-permute-start | bytes 200 | tf_op jit(solution)/shard_map/while/body/eval_jaxpr/ppermute | solution.py:11
  251.0 17.0 %collective-permute-start = (bf16[32,12288]{1,0:T(8,128)(2,1)S(1)}, bf16[32,12288]{1,0:T(8,128)(2,1)S(1)}, u32[]{:S(2)}, u32[]{:S(2)}) collective-permute-start(bf16[32,12288]{1,0:T(8,128)(2,1)S(1)} %get-tuple-element.264), channel_id=1, source_target_pairs={{0,2},{2,4},{4,6},{6,8},{8,10},{10,12},{12,14},{14,0},{1,3},{3,5},... | collective-permute-start | bytes 2359304 | tf_op jit(solution)/shard_map/while/body/eval_jaxpr/ppermute | solution.py:11
  251.1 16.9 %collective-permute-start.1 = (bf16[32]{0:T(256)(128)(2,1)S(1)}, bf16[32]{0:T(256)(128)(2,1)S(1)}, u32[]{:S(2)}, u32[]{:S(2)}) collective-permute-start(bf16[32]{0:T(256)(128)(2,1)S(1)} %convert_element_type.52), channel_id=1, source_target_pairs={{0,2},{2,4},{4,6},{6,8},{8,10},{10,12},{12,14},{14,0},{1,3},{3,5},... | collective-permute-start | bytes 200 | tf_op jit(solution)/shard_map/while/body/eval_jaxpr/ppermute | solution.py:11
Sparse Core Ops, SparseCore 0:
  281.5 14.7 all-reduce.1
where the time goes:
time: 306 us; the launch traced here: 305 us
  waiting for transfers between devices  149 us (49%)
  matrix products  119 us (39%)
  between operations  13.5 us (4%)
  local copies, waits for them, and re-layouts  9.01 us (3%)
  starting transfers between devices  6.17 us (2%)
  other arithmetic  5.66 us (2%)
    ppermute x14, waiting for transfers between devices, from_behind(): lax.ppermute(array, axis, [(i, (i + by) % devices) for i in range(devices)])  134 us
    dot_general x8, matrix products, record(): lax.dot_general(doc_grads, arrived, (((1,), (1,)), ((), ())), preferred_e...  97.9 us
    psum x1, waiting for transfers between devices, shards(): totals = lax.psum(scores.astype(jnp.bfloat16), 'mods').astype(jnp.float32)  14.8 us
    dot_general x1, matrix products, precondition(): mapped = jnp.einsum('qmij,mbj->qmib', scaled, basis_out, precision=high)  9.09 us
    ppermute x14, starting transfers between devices, from_behind(): lax.ppermute(array, axis, [(i, (i + by) % devices) for i in range(devices)])  6.17 us
  transfers between devices with their start and end apart: 15, of which 8 were waited for; matrix products, arithmetic and copies ran while one was open for 0% of the time, Pallas kernels for 0%

commit v1 on v0

v1 whole, which is shorter than its diff:
```python
import jax
import jax.numpy as jnp
from jax import lax
from jax.sharding import PartitionSpec as P

ref_tokens = 1024.0
bf16, f32 = jnp.bfloat16, jnp.float32


def precondition(gradient, basis_in, basis_out, eigen):
    high = lax.Precision.HIGH
    rotated = jnp.einsum("qab,bj->qaj", gradient, basis_out, precision=high)
    rotated = jnp.einsum("qaj,ai->qij", rotated, basis_in, precision=high)
    damping = 0.1 * jnp.mean(eigen)
    scaled = rotated / (eigen + damping)
    self_score = jnp.sum(rotated * scaled, axis=(1, 2))
    mapped = jnp.einsum("qij,ai->qaj", scaled, basis_in, precision=high)
    mapped = jnp.einsum("qaj,bj->qab", mapped, basis_out, precision=high)
    return mapped, self_score


def shards(doc_grads, query_grads, basis_in, basis_out, eigen, token_counts):
    queries_here = query_grads.shape[0]
    mods_here = basis_in.shape[0]
    width = basis_in.shape[1]
    size = width * width
    mods = lax.axis_size("mods")
    me_mod = lax.axis_index("mods")
    self_part = jnp.zeros((queries_here,), f32)
    scores = None
    for m in range(mods_here):
        gradient = query_grads[:, m * size : (m + 1) * size]
        gradient = gradient.reshape(queries_here, width, width).astype(f32)
        mapped, self_m = precondition(gradient, basis_in[m], basis_out[m], eigen[m])
        self_part = self_part + self_m
        block = mapped.reshape(queries_here, size).astype(bf16)
        if m == mods_here - 1:
            upper = self_part.astype(bf16)
            lower = (self_part - upper.astype(f32)).astype(bf16)
            pair = jnp.pad(jnp.stack([upper, lower], axis=1), ((0, 0), (0, 126)))
            block = jnp.concatenate([block, pair], axis=1)
        every = lax.all_gather(block, "docs", axis=0, tiled=True)
        part = lax.dot_general(
            doc_grads[:, m * size : (m + 1) * size],
            every[:, :size],
            (((1,), (1,)), ((), ())),
            preferred_element_type=f32,
        )
        scores = part if scores is None else scores + part
    pair = every[:, size : size + 2].T
    rows = [jnp.where(me_mod == k, pair, jnp.zeros_like(pair)) for k in range(mods)]
    totals = lax.psum(jnp.concatenate([scores.astype(bf16)] + rows, axis=0), "mods")
    docs_here = doc_grads.shape[0]
    self_terms = jnp.sum(totals[docs_here:].astype(f32), axis=0)
    factor = ref_tokens / token_counts.astype(f32)
    return totals[:docs_here].astype(f32) * lax.rsqrt(self_terms)[None, :] * factor[:, None]


def solution(mesh):
    in_specs = (
        P(("groups", "docs"), "mods"),
        P(("groups", "docs"), "mods"),
        P("mods", None, None),
        P("mods", None, None),
        P("mods", None, None),
        P(("groups", "docs")),
    )
    out_specs = P(("groups", "docs"), None)
    return jax.shard_map(shards, mesh=mesh, in_specs=in_specs, out_specs=out_specs, check_vma=False)
```

time: 306 us -> 207 us (0.68)
  matrix products: 119 us -> 31.3 us
  starting transfers between devices: 6.17 us -> 0.31 us
  waiting for transfers between devices: 149 us -> 145 us
    ppermute x14 -> x0, waiting for transfers between devices: 134 us -> none  [from_behind(): lax.ppermute(array, axis, [(i, (i + by) % devices) for i in range(devices)])]
    all_gather x0 -> x3, waiting for transfers between devices: none -> 128 us  [shards(): every = lax.all_gather(block, 'docs', axis=0, tiled=True)]
    dot_general x12 -> x15, matrix products: 119 us -> 31.3 us  [the longest x3 19.1 us: shards(): lax.dot_general(doc_grads[:, m * size:(m + 1) * size], every[:, :size], (...]
    ppermute x14 -> x0, starting transfers between devices: 6.17 us -> none  [from_behind(): lax.ppermute(array, axis, [(i, (i + by) % devices) for i in range(devices)])]
  transfers between devices with their start and end apart: 15 -> 4, of which waited for: 8 -> 4; matrix products, arithmetic and copies ran while one was open for 0% -> 12% of each run, Pallas kernels for 0% -> 0%
where the time goes in v1:
time: 207 us
  waiting for transfers between devices  145 us (70%)
  matrix products  31.3 us (15%)
  between operations  15.2 us (7%)
  local copies, waits for them, and re-layouts  8.24 us (4%)
  other arithmetic  6.12 us (3%)
    all_gather x3, waiting for transfers between devices, shards(): every = lax.all_gather(block, 'docs', axis=0, tiled=True)  128 us
    dot_general x3, matrix products, shards(): lax.dot_general(doc_grads[:, m * size:(m + 1) * size], every[:, :size], (...  19.1 us
    psum x1, waiting for transfers between devices, shards(): lax.psum(jnp.concatenate([scores.astype(bf16)] + rows, axis=0), 'mods')  17.5 us
    dot_general x3, matrix products, precondition(): mapped = jnp.einsum('qij,ai->qaj', scaled, basis_in, precision=high)  4.89 us
  transfers between devices with their start and end apart: 4, of which 4 were waited for; matrix products, arithmetic and copies ran while one was open for 12% of the time, Pallas kernels for 0%

profile of v1, /device:TPU:0, one launch (start us, length us, event | category | flops | bytes accessed | tf_op | source)
XLA Modules:
  0.0 206.5 jit_solution(8234694233263749859)
XLA Ops:
  6.5 0.0 copy-start
  6.5 0.0 copy-start.2
  6.5 0.0 all-gather.6.cloned.1.call-start
  6.5 1.5 slice_reduce_fusion
  10.0 0.8 add_bitcast_fusion
  10.8 0.1 copy.14
  10.8 1.2 fusion.61
  12.0 0.5 reshape.64
  12.6 0.0 copy-done
  12.6 1.1 fusion.41
  13.7 0.0 copy-done.2
  13.7 0.7 multiply_reduce_fusion.1
  14.4 1.6 convolution_bitcast_fusion.2
  16.0 0.6 convolution_convert_fusion.1
  16.6 1.2 convert_element_type.75
  17.8 0.0 all-gather.6.cloned.1.call-update
  17.8 0.0 all-gather.4.cloned.1.call-start
  17.9 0.1 copy.13
  18.0 0.5 reshape.63
  18.5 1.1 fusion.46
  19.7 0.7 multiply_reduce_fusion.2
  20.4 1.6 convolution_bitcast_fusion.4
  22.0 0.6 convolution_convert_fusion.2
  22.6 1.2 convert_element_type.73
  23.8 0.0 all-gather.4.cloned.1.call-update
  23.8 0.0 all-gather.8.cloned.1.call-start
  23.8 0.1 copy.15
  23.9 0.5 reshape.65
  24.5 1.1 fusion.36
  25.6 0.7 multiply_reduce_fusion
  26.3 0.1 copy.16
  26.4 1.6 convolution_bitcast_fusion
  28.1 0.6 convolution_convert_fusion
  28.7 0.5 convert_element_type.77
  29.1 0.7 fusion.32
  29.9 0.0 all-gather.8.cloned.1.call-update
  29.9 0.2 all-reduce.3.cloned.1.call-start
  30.1 40.0 %all-gather.6.cloned.1.call-done = bf16[256,4096]{1,0:T(8,128)(2,1)} async-done(((bf16[32,4096]{1,0:T(8,128)(2,1)}), bf16[256,4096]{1,0:T(8,128)(2,1)}) %all-gather.6.cloned.1.call-update) | async-done | bytes 2097168 | tf_op jit(solution)/shard_map/all_gather | solution.py:42
  70.1 6.4 %fusion.2 = f32[256,1024]{1,0:T(8,128)S(1)} fusion(bf16[256,4096]{1,0:T(8,128)(2,1)} %all-gather.6.cloned.1.call-done, bf16[1024,12288]{1,0:T(8,128)(2,1)} %param.6), kind=kOutput, calls=%fused_computation.2 | convolution fusion | flops 2147483648 | bytes 11534336 | tf_op jit(solution)/shard_map/dot_general | solution.py:43
  76.5 43.5 %all-gather.4.cloned.1.call-done = bf16[256,4096]{1,0:T(8,128)(2,1)} async-done(((bf16[32,4096]{1,0:T(8,128)(2,1)}), bf16[256,4096]{1,0:T(8,128)(2,1)}) %all-gather.4.cloned.1.call-update) | async-done | bytes 2097168 | tf_op jit(solution)/shard_map/all_gather | solution.py:42
  120.1 6.4 %fusion.7 = f32[256,1024]{1,0:T(8,128)S(1)} fusion(f32[256,1024]{1,0:T(8,128)S(1)} %fusion.2, bf16[256,4096]{1,0:T(8,128)(2,1)} %all-gather.4.cloned.1.call-done, bf16[1024,12288]{1,0:T(8,128)(2,1)} %param.6), kind=kOutput, calls=%fused_computation.13 | convolution fusion | flops 2147745792 | bytes 12582912 | tf_op jit(solution)/shard_map/dot_general | solution.py:43
  126.5 0.0 copy-start.1
  126.5 44.3 %all-gather.8.cloned.1.call-done = bf16[256,4224]{1,0:T(8,128)(2,1)} async-done(((bf16[32,4224]{1,0:T(8,128)(2,1)}), bf16[256,4224]{1,0:T(8,128)(2,1)}) %all-gather.8.cloned.1.call-update) | async-done | bytes 2162704 | tf_op jit(solution)/shard_map/all_gather | solution.py:42
  170.8 6.4 %fusion.20 = bf16[1024,256]{0,1:T(8,128)(2,1)S(1)} fusion(f32[256,1024]{1,0:T(8,128)S(1)} %fusion.7, bf16[1024,12288]{1,0:T(8,128)(2,1)} %param.6, bf16[256,4224]{1,0:T(8,128)(2,1)} %all-gather.8.cloned.1.call-done), kind=kOutput, calls=%fused_computation.19 | convolution fusion | flops 2148007936 | bytes 12058624 | tf_op jit(solution)/shard_map/dot_general | solution.py:43
  177.1 0.9 select_bitcast_fusion
  178.0 1.0 concatenate.7
  179.0 0.0 all-reduce.3.cloned.1.call-update
  179.0 0.0 copy-done.1
  179.0 17.5 %all-reduce.3.cloned.1.call-done = bf16[1028,256]{0,1:T(8,128)(2,1)} async-done(((bf16[1028,256]{0,1:T(8,128)(2,1)}), bf16[1028,256]{0,1:T(8,128)(2,1)}) %all-reduce.3.cloned.1.call-update) | async-done | bytes 526352 | tf_op jit(solution)/shard_map/psum | solution.py:52
  196.5 0.9 convert_reduce_fusion
  197.4 1.2 multiply_multiply_fusion
  198.7 1.3 copy.17
  (5 shorter events, 0.0 us)
Async XLA Ops:
  6.5 6.0 %copy-start = (f32[3,64,64]{2,1,0:T(8,128)S(1)}, f32[3,64,64]{2,1,0:T(8,128)}, u32[]{:S(2)}) copy-start(f32[3,64,64]{2,1,0:T(8,128)} %param.9) | copy-start | bytes 147460
  6.5 7.2 %copy-start.2 = (f32[3,64,64]{2,1,0:T(8,128)S(1)}, f32[3,64,64]{2,1,0:T(8,128)}, u32[]{:S(2)}) copy-start(f32[3,64,64]{2,1,0:T(8,128)} %param.8) | copy-start | bytes 147460
  6.5 63.6 %all-gather.6.cloned.1.call-start = ((), (), s32[]{:S(2)}) async-start(), calls=%async_computation.1 | async-start | bytes 2359296 | tf_op jit(solution)/shard_map/all_gather | solution.py:42
  17.8 102.2 %all-gather.4.cloned.1.call-start = ((), (), s32[]{:S(2)}) async-start(), calls=%async_computation | async-start | bytes 2359296 | tf_op jit(solution)/shard_map/all_gather | solution.py:42
  23.8 147.0 %all-gather.8.cloned.1.call-start = ((), (), s32[]{:S(2)}) async-start(), calls=%async_computation.2 | async-start | bytes 2433024 | tf_op jit(solution)/shard_map/all_gather | solution.py:42
  29.9 166.6 %all-reduce.3.cloned.1.call-start = ((), (), s32[]{:S(2)}) async-start(), calls=%async_computation.3 | async-start | bytes 1179648 | tf_op jit(solution)/shard_map/psum | solution.py:52
  126.5 52.5 %copy-start.1 = (s32[1024]{0:T(1024)S(1)}, s32[1024]{0:T(1024)}, u32[]{:S(2)}) copy-start(s32[1024]{0:T(1024)} %param.11) | copy-start | bytes 12292
Sparse Core Ops, SparseCore 0:
  18.0 52.1 all-gather.5
  72.3 47.7 all-gather.3
  122.3 48.4 all-gather.7
  179.1 17.3 all-reduce.2

commit v2 on v1

v2 whole, which is shorter than its diff:
```python
import functools

import jax
import jax.numpy as jnp
from jax import lax
from jax.experimental import pallas as pl
from jax.experimental.pallas import tpu as pltpu
from jax.sharding import PartitionSpec as P

ref_tokens = 1024.0
bf16, f32 = jnp.bfloat16, jnp.float32
MESH = pl.DeviceIdType.MESH
NT = (((1,), (1,)), ((), ()))


def precondition(gradient, basis_in, basis_out, eigen):
    high = lax.Precision.HIGH
    rotated = jnp.einsum("qab,bj->qaj", gradient, basis_out, precision=high)
    rotated = jnp.einsum("qaj,ai->qij", rotated, basis_in, precision=high)
    damping = 0.1 * jnp.mean(eigen)
    scaled = rotated / (eigen + damping)
    self_score = jnp.sum(rotated * scaled, axis=(1, 2))
    mapped = jnp.einsum("qij,ai->qaj", scaled, basis_in, precision=high)
    mapped = jnp.einsum("qaj,bj->qab", mapped, basis_out, precision=high)
    return mapped, self_score


def kernel(
    n, pair, chunks, tiles, blk, docs, factor, out, got, docs_v, acc, mine, theirs, selfs,
    their_selfs, send_sem, recv_sem, doc_sem, ex_send, ex_recv,
):
    me = lax.axis_index("docs")
    core = lax.axis_index("mods")
    z = lax.div(me, pair)
    y = lax.rem(me, pair)
    depth = n // pair
    up, down = me + pair, me - pair
    beside = z * pair + (pair - 1 - y)
    has_up, has_down = z < depth - 1, z > 0
    q = blk.shape[0]
    wide = blk.shape[1]
    features = docs.shape[1]
    part = features // chunks
    tile = docs.shape[0] // tiles

    def load(c):
        cols = pl.ds(c * part, part)
        return pltpu.make_async_copy(docs.at[:, cols], docs_v.at[:, cols], doc_sem.at[c])

    for c in range(chunks):
        load(c).start()

    barrier = pltpu.get_barrier_semaphore()
    for yes, to in ((has_up, up), (has_down, down)):

        @pl.when(yes)
        def _(to=to):
            pl.semaphore_signal(barrier, inc=1, device_id={"docs": to}, device_id_type=MESH)

    if pair > 1:
        pl.semaphore_signal(barrier, inc=1, device_id={"docs": beside}, device_id_type=MESH)
    pl.semaphore_signal(barrier, inc=1, device_id={"mods": 1 - core}, device_id_type=MESH)
    peers = 2 if pair > 1 else 1
    line_peers = has_up.astype(jnp.int32) + has_down.astype(jnp.int32)
    pl.semaphore_wait(barrier, peers + line_peers)

    def piece(source, c):
        start = c * part
        stop = (c + 1) * part if c < chunks - 1 else wide
        return (pl.ds(pl.multiple_of(source * q, q), q), pl.ds(start, stop - start))

    def copy(way, source, c, own=False):
        rows, cols = piece(source, c)
        to = (up, down, beside)[way]
        return pltpu.make_async_remote_copy(
            src_ref=blk.at[:, cols] if own else got.at[rows, cols],
            dst_ref=got.at[rows, cols],
            send_sem=send_sem.at[way, source, c],
            recv_sem=recv_sem.at[source, c],
            device_id={"docs": to},
            device_id_type=MESH,
        )

    def own_each(c, act):
        @pl.when(has_up)
        def _():
            act(copy(0, me, c, True))

        @pl.when(has_down)
        def _():
            act(copy(1, me, c, True))

        if pair > 1:
            act(copy(2, me, c, True))

    def line_each(c, wait):
        for d in range(1, depth):

            @pl.when(z >= d)
            def _():
                source = me - d * pair
                if wait:
                    copy(0, source, c).wait_recv()

                @pl.when(has_up)
                def _():
                    one = copy(0, source, c)
                    one.start() if wait else one.wait_send()

                if pair > 1:
                    one = copy(2, source, c)
                    one.start() if wait else one.wait_send()

            @pl.when(z + d < depth)
            def _():
                source = me + d * pair
                if wait:
                    copy(1, source, c).wait_recv()

                @pl.when(has_down)
                def _():
                    one = copy(1, source, c)
                    one.start() if wait else one.wait_send()

                if pair > 1:
                    one = copy(2, source, c)
                    one.start() if wait else one.wait_send()

    def beside_wait(c):
        if pair > 1:
            for level in range(depth):
                copy(2, level * pair + (pair - 1 - y), c).wait_recv()

    def product(c, t):
        rows = pl.ds(t * tile, tile)
        cols = pl.ds(c * part, part)
        value = lax.dot_general(docs_v[rows, cols], got[:, cols], NT, preferred_element_type=f32)
        if c == 0:
            acc[rows, :] = value
            return value
        return acc[rows, :] + value

    for c in range(min(2, chunks)):
        own_each(c, lambda one: one.start())
    got[pl.ds(pl.multiple_of(me * q, q), q), :] = blk[...]
    for c in range(chunks):
        line_each(c, True)
        if c + 2 < chunks:
            own_each(c + 2, lambda one: one.start())
        if c >= 1:
            beside_wait(c - 1)
            load(c - 1).wait()
            for t in range(tiles):
                value = product(c - 1, t)
                if c > 1:
                    acc[pl.ds(t * tile, tile), :] = value

    last = chunks - 1
    beside_wait(last)
    load(last).wait()

    def swap(t):
        if t == tiles:
            src, dst = selfs, their_selfs
        else:
            rows = pl.ds(t * tile, tile)
            src, dst = mine.at[rows, :], theirs.at[rows, :]
        return pltpu.make_async_remote_copy(
            src_ref=src,
            dst_ref=dst,
            send_sem=ex_send.at[t],
            recv_sem=ex_recv.at[t],
            device_id={"mods": 1 - core},
            device_id_type=MESH,
        )

    lane = lax.broadcasted_iota(jnp.int32, (16, wide - features), 1)
    pick = jnp.where(lane < 2, 1.0, 0.0).astype(bf16)
    selfs[...] = lax.dot_general(
        pick, got[:, pl.ds(features, wide - features)], NT, preferred_element_type=f32
    )
    swap(tiles).start()
    for t in range(tiles):
        mine[pl.ds(t * tile, tile), :] = product(last, t).astype(bf16)
        swap(t).start()
    swap(tiles).wait()
    scale = lax.rsqrt(selfs[0:1, :] + their_selfs[0:1, :])
    for t in range(tiles):
        rows = pl.ds(t * tile, tile)
        swap(t).wait()
        total = mine[rows, :].astype(f32) + theirs[rows, :].astype(f32)
        out[rows, :] = total * scale * factor[rows, :]
    for c in range(chunks):
        own_each(c, lambda one: one.wait_send())
        line_each(c, False)


def gather_and_score(n, pair, chunks, block, docs, factor):
    q, wide = block.shape
    rows, features = docs.shape
    queries, tiles = n * q, 4
    vmem = pl.BlockSpec(memory_space=pltpu.VMEM)
    return pl.pallas_call(
        functools.partial(kernel, n, pair, chunks, tiles),
        out_shape=jax.ShapeDtypeStruct((rows, queries), f32),
        in_specs=[vmem, pl.BlockSpec(memory_space=pl.ANY), vmem],
        out_specs=vmem,
        scratch_shapes=[
            pltpu.VMEM((queries, wide), bf16),
            pltpu.VMEM((rows, features), bf16),
            pltpu.VMEM((rows, queries), f32),
            pltpu.VMEM((rows, queries), bf16),
            pltpu.VMEM((rows, queries), bf16),
            pltpu.VMEM((16, queries), f32),
            pltpu.VMEM((16, queries), f32),
            pltpu.SemaphoreType.DMA((3, n, chunks)),
            pltpu.SemaphoreType.DMA((n, chunks)),
            pltpu.SemaphoreType.DMA((chunks,)),
            pltpu.SemaphoreType.DMA((tiles + 1,)),
            pltpu.SemaphoreType.DMA((tiles + 1,)),
        ],
        compiler_params=pltpu.CompilerParams(
            collective_id=0, has_side_effects=True, vmem_limit_bytes=52 << 20
        ),
        cost_estimate=pl.CostEstimate(
            flops=2 * rows * features * queries,
            bytes_accessed=2 * rows * features,
            transcendentals=0,
        ),
    )(block, docs, factor)


def shards(n, pair, doc_grads, query_grads, basis_in, basis_out, eigen, token_counts):
    queries_here = query_grads.shape[0]
    mods_here = basis_in.shape[0]
    width = basis_in.shape[1]
    size = width * width
    self_part = jnp.zeros((queries_here,), f32)
    blocks = []
    for m in range(mods_here):
        gradient = query_grads[:, m * size : (m + 1) * size]
        gradient = gradient.reshape(queries_here, width, width).astype(f32)
        mapped, self_m = precondition(gradient, basis_in[m], basis_out[m], eigen[m])
        self_part = self_part + self_m
        blocks.append(mapped.reshape(queries_here, size).astype(bf16))
    upper = self_part.astype(bf16)
    lower = (self_part - upper.astype(f32)).astype(bf16)
    blocks.append(jnp.pad(jnp.stack([upper, lower], axis=1), ((0, 0), (0, 126))))
    block = jnp.concatenate(blocks, axis=1)
    factor = (ref_tokens / token_counts.astype(f32))[:, None]
    return gather_and_score(n, pair, mods_here, block, doc_grads, factor)


def solution(mesh):
    n = mesh.shape["docs"]
    pair = 2 if mesh.shape["groups"] == 2 and n % 2 == 0 else 1
    in_specs = (
        P(("groups", "docs"), "mods"),
        P(("groups", "docs"), "mods"),
        P("mods", None, None),
        P("mods", None, None),
        P("mods", None, None),
        P(("groups", "docs")),
    )
    out_specs = P(("groups", "docs"), None)
    body = functools.partial(shards, n, pair)
    return jax.shard_map(body, mesh=mesh, in_specs=in_specs, out_specs=out_specs, check_vma=False)
```

time: 207 us -> 105 us (0.51)
  waiting for transfers between devices: 145 us -> 0 us
  Pallas kernels: 0 us -> 83.5 us
  matrix products: 31.3 us -> 10.2 us
  between operations: 15.2 us -> 2.06 us
  other arithmetic: 6.12 us -> 3.14 us
  local copies, waits for them, and re-layouts: 8.24 us -> 5.89 us
    all_gather x3 -> x0, waiting for transfers between devices: 128 us -> none  [shards(): every = lax.all_gather(block, 'docs', axis=0, tiled=True)]
    pallas_call x0 -> x1, Pallas kernels: none -> 83.5 us  [gather_and_score(): pl.pallas_call(functools.partial(kernel, n, pair, chunks, tiles), out_sha...]
    dot_general x3 -> x0, matrix products: 19.1 us -> none  [shards(): lax.dot_general(doc_grads[:, m * size:(m + 1) * size], every[:, :size], (...]
    psum x1 -> x0, waiting for transfers between devices: 17.5 us -> none  [shards(): lax.psum(jnp.concatenate([scores.astype(bf16)] + rows, axis=0), 'mods')]
    dot_general x3, matrix products: 4.89 us -> 1.74 us  [precondition(): mapped = jnp.einsum('qij,ai->qaj', scaled, basis_in, precision=high)]
    unnamed x6 -> x7, local copies, waits for them, and re-layouts: 0.01 us -> 2.28 us
  transfers between devices with their start and end apart: 4 -> 0, of which waited for: 4 -> 0; matrix products, arithmetic and copies ran while one was open for 12% -> 0% of each run, Pallas kernels for 0% -> 0%
where the time goes in v2:
time: 105 us
  Pallas kernels  83.5 us (80%)
  matrix products  10.2 us (10%)
  local copies, waits for them, and re-layouts  5.89 us (6%)
  other arithmetic  3.14 us (3%)
  between operations  2.06 us (2%)
    pallas_call x1, Pallas kernels, gather_and_score(): pl.pallas_call(functools.partial(kernel, n, pair, chunks, tiles), out_sha...  83.5 us
    dot_general x3, matrix products, precondition(): rotated = jnp.einsum('qab,bj->qaj', gradient, basis_out, precision=high)  3.42 us
    dot_general x3, matrix products, precondition(): mapped = jnp.einsum('qaj,bj->qab', mapped, basis_out, precision=high)  2.98 us
    unnamed x7, local copies, waits for them, and re-layouts  2.28 us

profile of v2, /device:TPU:0, one launch (start us, length us, event | category | flops | bytes accessed | tf_op | source)
XLA Modules:
  0.0 104.9 jit_solution(3174289593061947468)
XLA Ops:
  0.0 0.0 copy-start
  0.0 1.6 %slice_reduce_fusion.1 = (f32[]{:T(128)}, f32[]{:T(128)}, f32[]{:T(128)}) fusion(f32[3,64,64]{2,1,0:T(8,128)} %param.10), kind=kLoop, calls=%fused_computation.44 | loop fusion | flops 12285 | bytes 49164 | tf_op jit(solution)/shard_map/reduce_sum | solution.py:20
  3.5 0.7 convert_divide_fusion
  4.2 0.8 add_bitcast_fusion.1
  5.0 0.0 copy-start.1
  5.0 0.1 copy.22
  5.0 0.1 copy.25
  5.1 0.1 copy.19
  5.2 0.2 copy.28.factor
  5.5 0.0 copy-done
  5.5 0.1 fusion.36
  5.5 0.0 copy-start.2
  5.5 0.5 reshape.60
  6.1 0.0 copy-done.1
  6.1 1.1 %fusion.16 = f32[32,64,64]{1,2,0:T(8,128)S(1)} fusion(bf16[32,64,64]{2,1,0:T(8,128)(2,1)S(1)} %reshape.60, f32[3,64,64]{2,1,0:T(8,128)S(1)} %copy-done.1), kind=kOutput, calls=%fused_computation.29 | convolution fusion | flops 50331648 | bytes 1081344 | tf_op jit(solution)/shard_map/qab,bj->qaj/dot_general | solution.py:18
  7.2 0.0 copy-done.2
  7.2 0.7 multiply_reduce_fusion.1
  7.9 0.6 convolution_bitcast_fusion.2
  8.5 1.0 convolution_convert_fusion.1
  9.5 0.5 convert_element_type.63
  10.0 0.5 reshape.59
  10.5 1.1 %fusion.21 = f32[32,64,64]{1,2,0:T(8,128)S(1)} fusion(bf16[32,64,64]{2,1,0:T(8,128)(2,1)S(1)} %reshape.59, f32[3,64,64]{2,1,0:T(8,128)S(1)} %copy-done.1), kind=kOutput, calls=%fused_computation.34 | convolution fusion | flops 50331648 | bytes 1081344 | tf_op jit(solution)/shard_map/qab,bj->qaj/dot_general | solution.py:18
  11.7 0.7 multiply_reduce_fusion.2
  12.4 0.6 convolution_bitcast_fusion.4
  13.0 1.0 convolution_convert_fusion.2
  14.0 0.5 convert_element_type.61
  14.4 0.5 reshape.61
  15.0 1.1 %fusion.11 = f32[32,64,64]{1,2,0:T(8,128)S(1)} fusion(bf16[32,64,64]{2,1,0:T(8,128)(2,1)S(1)} %reshape.61, f32[3,64,64]{2,1,0:T(8,128)S(1)} %copy-done.1), kind=kOutput, calls=%fused_computation.24 | convolution fusion | flops 50331648 | bytes 1081344 | tf_op jit(solution)/shard_map/qab,bj->qaj/dot_general | solution.py:18
  16.1 0.7 multiply_reduce_fusion
  16.8 0.6 convolution_bitcast_fusion
  17.4 1.0 convolution_convert_fusion
  18.4 0.5 convert_element_type.65
  18.9 0.1 copy.27
  19.0 0.1 fusion.4.blk
  19.1 83.5 %shard_map.64 = f32[1024,256]{1,0:T(8,128)} custom-call(bf16[32,12416]{1,0:T(8,128)(2,1)S(1)} %fusion.4.blk, bf16[1024,12288]{1,0:T(8,128)(2,1)} %docs.1, f32[1024,1]{1,0:T(8,128)S(1)} %copy.28.factor), custom_call_target="tpu_custom_call" | custom-call | flops 6442450944 | bytes 25165824 | tf_op jit(solution)/shard_map/pallas_call | solution.py:203
  102.6 2.3 %copy.36 = f32[1024,256]{1,0:T(8,128)} copy(f32[1024,256]{1,0:T(8,128)} %shard_map.64) | data formatting | bytes 2097152
  (3 shorter events, 0.0 us)
Async XLA Ops:
  0.0 5.5 %copy-start = (bf16[32,12288]{1,0:T(8,128)(2,1)S(1)}, bf16[32,12288]{1,0:T(8,128)(2,1)}, u32[]{:S(2)}) copy-start(bf16[32,12288]{1,0:T(8,128)(2,1)} %param.7) | copy-start | bytes 2359300
  5.0 1.1 %copy-start.1 = (f32[3,64,64]{2,1,0:T(8,128)S(1)}, f32[3,64,64]{2,1,0:T(8,128)}, u32[]{:S(2)}) copy-start(f32[3,64,64]{2,1,0:T(8,128)} %param.9) | copy-start | bytes 147460
  5.5 1.7 %copy-start.2 = (f32[3,64,64]{2,1,0:T(8,128)S(1)}, f32[3,64,64]{2,1,0:T(8,128)}, u32[]{:S(2)}) copy-start(f32[3,64,64]{2,1,0:T(8,128)} %param.8) | copy-start | bytes 147460

commit v3 on v2

--- a/solution.py
+++ b/solution.py
@@ -26,7 +26,7 @@
 
 
 def kernel(
-    n, pair, chunks, tiles, blk, docs, factor, out, got, docs_v, acc, mine, theirs, selfs,
+    n, pair, tiles, blk, docs, factor, out, got, docs_v, acc, mine, theirs, selfs,
     their_selfs, send_sem, recv_sem, doc_sem, ex_send, ex_recv,
 ):
     me = lax.axis_index("docs")
@@ -40,11 +40,13 @@
     q = blk.shape[0]
     wide = blk.shape[1]
     features = docs.shape[1]
-    part = features // chunks
+    third = features // 3
+    edges = (0, third, 2 * third, 2 * third + third // 4 * 3, features)
+    chunks = len(edges) - 1
     tile = docs.shape[0] // tiles
 
     def load(c):
-        cols = pl.ds(c * part, part)
+        cols = pl.ds(edges[c], edges[c + 1] - edges[c])
         return pltpu.make_async_copy(docs.at[:, cols], docs_v.at[:, cols], doc_sem.at[c])
 
     for c in range(chunks):
@@ -64,76 +66,86 @@
     line_peers = has_up.astype(jnp.int32) + has_down.astype(jnp.int32)
     pl.semaphore_wait(barrier, peers + line_peers)
 
-    def piece(source, c):
-        start = c * part
-        stop = (c + 1) * part if c < chunks - 1 else wide
+    both = pair > 1
+
+    def piece(source, k):
+        c = k // 2
+        start, stop = edges[c], edges[c + 1] if c < chunks - 1 else wide
+        cut = stop - (stop - start) * 5 // 32 // 128 * 128 if both else stop
+        start, stop = (start, cut) if k % 2 == 0 else (cut, stop)
         return (pl.ds(pl.multiple_of(source * q, q), q), pl.ds(start, stop - start))
 
-    def copy(way, source, c, own=False):
-        rows, cols = piece(source, c)
+    def copy(way, source, k, own=False):
+        rows, cols = piece(source, k)
         to = (up, down, beside)[way]
         return pltpu.make_async_remote_copy(
             src_ref=blk.at[:, cols] if own else got.at[rows, cols],
             dst_ref=got.at[rows, cols],
-            send_sem=send_sem.at[way, source, c],
-            recv_sem=recv_sem.at[source, c],
+            send_sem=send_sem.at[way, source, k],
+            recv_sem=recv_sem.at[source, k],
             device_id={"docs": to},
             device_id_type=MESH,
         )
 
-    def own_each(c, act):
-        @pl.when(has_up)
-        def _():
-            act(copy(0, me, c, True))
-
-        @pl.when(has_down)
-        def _():
-            act(copy(1, me, c, True))
-
-        if pair > 1:
-            act(copy(2, me, c, True))
-
-    def line_each(c, wait):
+    lines = ((has_up, 0), (has_down, 1))
+
+    def act(one, first):
+        if first:
+            one.start()
+        else:
+            one.wait_send()
+
+    def own_each(c, first):
+        if both:
+            act(copy(2, me, 2 * c + 1, True), first)
+            act(copy(2, me, 2 * c, True), first)
+        for yes, way in lines:
+
+            @pl.when(yes)
+            def _(way=way):
+                act(copy(way, me, 2 * c, True), first)
+                if both:
+                    act(copy(way, me, 2 * c + 1, True), first)
+
+    def beside_each(c, first):
+        if both:
+            if first:
+                copy(2, beside, 2 * c + 1).wait_recv()
+            for yes, way in lines:
+
+                @pl.when(yes)
+                def _(way=way):
+                    act(copy(way, beside, 2 * c + 1), first)
+
+    def line_each(c, first):
+        beside_each(c, first)
         for d in range(1, depth):
-
-            @pl.when(z >= d)
-            def _():
-                source = me - d * pair
-                if wait:
-                    copy(0, source, c).wait_recv()
-
-                @pl.when(has_up)
-                def _():
-                    one = copy(0, source, c)
-                    one.start() if wait else one.wait_send()
-
-                if pair > 1:
-                    one = copy(2, source, c)
-                    one.start() if wait else one.wait_send()
-
-            @pl.when(z + d < depth)
-            def _():
-                source = me + d * pair
-                if wait:
-                    copy(1, source, c).wait_recv()
-
-                @pl.when(has_down)
-                def _():
-                    one = copy(1, source, c)
-                    one.start() if wait else one.wait_send()
-
-                if pair > 1:
-                    one = copy(2, source, c)
-                    one.start() if wait else one.wait_send()
+            for (onward, way), here, by in zip(lines, (z >= d, z + d < depth), (-d, d)):
+
+                @pl.when(here)
+                def _(onward=onward, way=way, by=by):
+                    moves = [(me + by * pair, 2 * c)]
+                    if both:
+                        moves += [(me + by * pair, 2 * c + 1), (beside + by * pair, 2 * c + 1)]
+                    for source, k in moves:
+                        if first:
+                            copy(way, source, k).wait_recv()
+
+                        @pl.when(onward)
+                        def _(source=source, k=k):
+                            act(copy(way, source, k), first)
+
+                        if both and k % 2 == 0:
+                            act(copy(2, source, k), first)
 
     def beside_wait(c):
-        if pair > 1:
+        if both:
             for level in range(depth):
-                copy(2, level * pair + (pair - 1 - y), c).wait_recv()
+                copy(2, level * pair + (pair - 1 - y), 2 * c).wait_recv()
 
     def product(c, t):
         rows = pl.ds(t * tile, tile)
-        cols = pl.ds(c * part, part)
+        cols = pl.ds(edges[c], edges[c + 1] - edges[c])
         value = lax.dot_general(docs_v[rows, cols], got[:, cols], NT, preferred_element_type=f32)
         if c == 0:
             acc[rows, :] = value
@@ -141,12 +153,12 @@
         return acc[rows, :] + value
 
     for c in range(min(2, chunks)):
-        own_each(c, lambda one: one.start())
+        own_each(c, True)
     got[pl.ds(pl.multiple_of(me * q, q), q), :] = blk[...]
     for c in range(chunks):
         line_each(c, True)
         if c + 2 < chunks:
-            own_each(c + 2, lambda one: one.start())
+            own_each(c + 2, True)
         if c >= 1:
             beside_wait(c - 1)
             load(c - 1).wait()
@@ -191,17 +203,17 @@
         total = mine[rows, :].astype(f32) + theirs[rows, :].astype(f32)
         out[rows, :] = total * scale * factor[rows, :]
     for c in range(chunks):
-        own_each(c, lambda one: one.wait_send())
+        own_each(c, False)
         line_each(c, False)
 
 
-def gather_and_score(n, pair, chunks, block, docs, factor):
+def gather_and_score(n, pair, block, docs, factor):
     q, wide = block.shape
     rows, features = docs.shape
     queries, tiles = n * q, 4
     vmem = pl.BlockSpec(memory_space=pltpu.VMEM)
     return pl.pallas_call(
-        functools.partial(kernel, n, pair, chunks, tiles),
+        functools.partial(kernel, n, pair, tiles),
         out_shape=jax.ShapeDtypeStruct((rows, queries), f32),
         in_specs=[vmem, pl.BlockSpec(memory_space=pl.ANY), vmem],
         out_specs=vmem,
@@ -213,9 +225,9 @@
             pltpu.VMEM((rows, queries), bf16),
             pltpu.VMEM((16, queries), f32),
             pltpu.VMEM((16, queries), f32),
-            pltpu.SemaphoreType.DMA((3, n, chunks)),
-            pltpu.SemaphoreType.DMA((n, chunks)),
-            pltpu.SemaphoreType.DMA((chunks,)),
+            pltpu.SemaphoreType.DMA((3, n, 8)),
+            pltpu.SemaphoreType.DMA((n, 8)),
+            pltpu.SemaphoreType.DMA((4,)),
             pltpu.SemaphoreType.DMA((tiles + 1,)),
             pltpu.SemaphoreType.DMA((tiles + 1,)),
         ],
@@ -248,7 +260,7 @@
     blocks.append(jnp.pad(jnp.stack([upper, lower], axis=1), ((0, 0), (0, 126))))
     block = jnp.concatenate(blocks, axis=1)
     factor = (ref_tokens / token_counts.astype(f32))[:, None]
-    return gather_and_score(n, pair, mods_here, block, doc_grads, factor)
+    return gather_and_score(n, pair, block, doc_grads, factor)
 
 
 def solution(mesh):

time: 105 us -> 103 us (0.981)
  Pallas kernels: 83.5 us -> 81.4 us
    pallas_call x1, Pallas kernels: 83.5 us -> 81.4 us  [gather_and_score(): pl.pallas_call(functools.partial(kernel, n, pair, tiles), out_shape=jax.S...]
where the time goes in v3:
time: 103 us
  Pallas kernels  81.4 us (79%)
  matrix products  10.2 us (10%)
  local copies, waits for them, and re-layouts  5.89 us (6%)
  other arithmetic  3.14 us (3%)
  between operations  2.06 us (2%)
    pallas_call x1, Pallas kernels, gather_and_score(): pl.pallas_call(functools.partial(kernel, n, pair, tiles), out_shape=jax.S...  81.4 us
    dot_general x3, matrix products, precondition(): rotated = jnp.einsum('qab,bj->qaj', gradient, basis_out, precision=high)  3.42 us
    dot_general x3, matrix products, precondition(): mapped = jnp.einsum('qaj,bj->qab', mapped, basis_out, precision=high)  2.98 us
    unnamed x7, local copies, waits for them, and re-layouts  2.28 us
    dot_general x3, matrix products, precondition(): rotated = jnp.einsum('qaj,ai->qij', rotated, basis_in, precision=high)  2.1 us

profile of v3, /device:TPU:0, one launch (start us, length us, event | category | flops | bytes accessed | tf_op | source)
XLA Modules:
  0.0 102.7 jit_solution(10709464125507656887)
XLA Ops:
  0.0 0.0 copy-start
  0.0 1.6 %slice_reduce_fusion.1 = (f32[]{:T(128)}, f32[]{:T(128)}, f32[]{:T(128)}) fusion(f32[3,64,64]{2,1,0:T(8,128)} %param.10), kind=kLoop, calls=%fused_computation.44 | loop fusion | flops 12285 | bytes 49164 | tf_op jit(solution)/shard_map/reduce_sum | solution.py:20
  3.5 0.7 convert_divide_fusion
  4.2 0.8 add_bitcast_fusion.1
  5.0 0.0 copy-start.1
  5.0 0.1 copy.22
  5.0 0.1 copy.25
  5.1 0.1 copy.19
  5.2 0.2 copy.28.factor
  5.5 0.0 copy-done
  5.5 0.1 fusion.36
  5.5 0.0 copy-start.2
  5.5 0.5 reshape.60
  6.1 0.0 copy-done.1
  6.1 1.1 %fusion.16 = f32[32,64,64]{1,2,0:T(8,128)S(1)} fusion(bf16[32,64,64]{2,1,0:T(8,128)(2,1)S(1)} %reshape.60, f32[3,64,64]{2,1,0:T(8,128)S(1)} %copy-done.1), kind=kOutput, calls=%fused_computation.29 | convolution fusion | flops 50331648 | bytes 1081344 | tf_op jit(solution)/shard_map/qab,bj->qaj/dot_general | solution.py:18
  7.2 0.0 copy-done.2
  7.2 0.7 multiply_reduce_fusion.1
  7.9 0.6 convolution_bitcast_fusion.2
  8.5 1.0 convolution_convert_fusion.1
  9.5 0.5 convert_element_type.63
  10.0 0.5 reshape.59
  10.5 1.1 %fusion.21 = f32[32,64,64]{1,2,0:T(8,128)S(1)} fusion(bf16[32,64,64]{2,1,0:T(8,128)(2,1)S(1)} %reshape.59, f32[3,64,64]{2,1,0:T(8,128)S(1)} %copy-done.1), kind=kOutput, calls=%fused_computation.34 | convolution fusion | flops 50331648 | bytes 1081344 | tf_op jit(solution)/shard_map/qab,bj->qaj/dot_general | solution.py:18
  11.7 0.7 multiply_reduce_fusion.2
  12.4 0.6 convolution_bitcast_fusion.4
  13.0 1.0 convolution_convert_fusion.2
  14.0 0.5 convert_element_type.61
  14.4 0.5 reshape.61
  15.0 1.1 %fusion.11 = f32[32,64,64]{1,2,0:T(8,128)S(1)} fusion(bf16[32,64,64]{2,1,0:T(8,128)(2,1)S(1)} %reshape.61, f32[3,64,64]{2,1,0:T(8,128)S(1)} %copy-done.1), kind=kOutput, calls=%fused_computation.24 | convolution fusion | flops 50331648 | bytes 1081344 | tf_op jit(solution)/shard_map/qab,bj->qaj/dot_general | solution.py:18
  16.1 0.7 multiply_reduce_fusion
  16.8 0.6 convolution_bitcast_fusion
  17.4 1.0 convolution_convert_fusion
  18.4 0.5 convert_element_type.65
  18.9 0.1 copy.27
  19.0 0.1 fusion.4.blk
  19.1 81.4 %shard_map.64 = f32[1024,256]{1,0:T(8,128)} custom-call(bf16[32,12416]{1,0:T(8,128)(2,1)S(1)} %fusion.4.blk, bf16[1024,12288]{1,0:T(8,128)(2,1)} %docs.1, f32[1024,1]{1,0:T(8,128)S(1)} %copy.28.factor), custom_call_target="tpu_custom_call" | custom-call | flops 6442450944 | bytes 25165824 | tf_op jit(solution)/shard_map/pallas_call | solution.py:215
  100.4 2.3 %copy.36 = f32[1024,256]{1,0:T(8,128)} copy(f32[1024,256]{1,0:T(8,128)} %shard_map.64) | data formatting | bytes 2097152
  (3 shorter events, 0.0 us)
Async XLA Ops:
  0.0 5.5 %copy-start = (bf16[32,12288]{1,0:T(8,128)(2,1)S(1)}, bf16[32,12288]{1,0:T(8,128)(2,1)}, u32[]{:S(2)}) copy-start(bf16[32,12288]{1,0:T(8,128)(2,1)} %param.7) | copy-start | bytes 2359300
  5.0 1.1 %copy-start.1 = (f32[3,64,64]{2,1,0:T(8,128)S(1)}, f32[3,64,64]{2,1,0:T(8,128)}, u32[]{:S(2)}) copy-start(f32[3,64,64]{2,1,0:T(8,128)} %param.9) | copy-start | bytes 147460
  5.5 1.7 %copy-start.2 = (f32[3,64,64]{2,1,0:T(8,128)S(1)}, f32[3,64,64]{2,1,0:T(8,128)}, u32[]{:S(2)}) copy-start(f32[3,64,64]{2,1,0:T(8,128)} %param.8) | copy-start | bytes 147460

commit v4 on v3

--- a/solution.py
+++ b/solution.py
@@ -88,6 +88,7 @@
         )
 
     lines = ((has_up, 0), (has_down, 1))
+    pending = []
 
     def act(one, first):
         if first:
@@ -138,6 +139,9 @@
                         if both and k % 2 == 0:
                             act(copy(2, source, k), first)
 
+            if first and pending:
+                pending.pop(0)()
+
     def beside_wait(c):
         if both:
             for level in range(depth):
@@ -152,20 +156,25 @@
             return value
         return acc[rows, :] + value
 
-    for c in range(min(2, chunks)):
+    def add(c, t):
+        value = product(c, t)
+        if c > 0:
+            acc[pl.ds(t * tile, tile), :] = value
+
+    for c in range(chunks):
         own_each(c, True)
     got[pl.ds(pl.multiple_of(me * q, q), q), :] = blk[...]
     for c in range(chunks):
         line_each(c, True)
-        if c + 2 < chunks:
-            own_each(c + 2, True)
+        while pending:
+            pending.pop(0)()
         if c >= 1:
             beside_wait(c - 1)
             load(c - 1).wait()
-            for t in range(tiles):
-                value = product(c - 1, t)
-                if c > 1:
-                    acc[pl.ds(t * tile, tile), :] = value
+            pending.extend(functools.partial(add, c - 1, t) for t in range(tiles))
+            pending.pop(0)()
+    while pending:
+        pending.pop(0)()
 
     last = chunks - 1
     beside_wait(last)

time: 103 us -> 104 us (level)
  Pallas kernels: 81.4 us -> 82.8 us
    pallas_call x1, Pallas kernels: 81.4 us -> 82.8 us  [gather_and_score(): pl.pallas_call(functools.partial(kernel, n, pair, tiles), out_shape=jax.S...]
where the time goes in v4:
time: 104 us
  Pallas kernels  82.8 us (80%)
  matrix products  10.2 us (10%)
  local copies, waits for them, and re-layouts  5.89 us (6%)
  other arithmetic  3.14 us (3%)
  between operations  2.06 us (2%)
    pallas_call x1, Pallas kernels, gather_and_score(): pl.pallas_call(functools.partial(kernel, n, pair, tiles), out_shape=jax.S...  82.8 us
    dot_general x3, matrix products, precondition(): rotated = jnp.einsum('qab,bj->qaj', gradient, basis_out, precision=high)  3.42 us
    dot_general x3, matrix products, precondition(): mapped = jnp.einsum('qaj,bj->qab', mapped, basis_out, precision=high)  2.98 us
    unnamed x7, local copies, waits for them, and re-layouts  2.28 us
    dot_general x3, matrix products, precondition(): rotated = jnp.einsum('qaj,ai->qij', rotated, basis_in, precision=high)  2.1 us

profile of v4, /device:TPU:0, one launch (start us, length us, event | category | flops | bytes accessed | tf_op | source)
XLA Modules:
  0.0 104.1 jit_solution(6527743859959783281)
XLA Ops:
  0.0 0.0 copy-start
  0.0 1.6 %slice_reduce_fusion.1 = (f32[]{:T(128)}, f32[]{:T(128)}, f32[]{:T(128)}) fusion(f32[3,64,64]{2,1,0:T(8,128)} %param.10), kind=kLoop, calls=%fused_computation.44 | loop fusion | flops 12285 | bytes 49164 | tf_op jit(solution)/shard_map/reduce_sum | solution.py:20
  3.5 0.7 convert_divide_fusion
  4.2 0.8 add_bitcast_fusion.1
  5.0 0.0 copy-start.1
  5.0 0.1 copy.22
  5.0 0.1 copy.25
  5.1 0.1 copy.19
  5.2 0.2 copy.28.factor
  5.5 0.0 copy-done
  5.5 0.1 fusion.36
  5.5 0.0 copy-start.2
  5.5 0.5 reshape.60
  6.1 0.0 copy-done.1
  6.1 1.1 %fusion.16 = f32[32,64,64]{1,2,0:T(8,128)S(1)} fusion(bf16[32,64,64]{2,1,0:T(8,128)(2,1)S(1)} %reshape.60, f32[3,64,64]{2,1,0:T(8,128)S(1)} %copy-done.1), kind=kOutput, calls=%fused_computation.29 | convolution fusion | flops 50331648 | bytes 1081344 | tf_op jit(solution)/shard_map/qab,bj->qaj/dot_general | solution.py:18
  7.2 0.0 copy-done.2
  7.2 0.7 multiply_reduce_fusion.1
  7.9 0.6 convolution_bitcast_fusion.2
  8.5 1.0 convolution_convert_fusion.1
  9.5 0.5 convert_element_type.63
  10.0 0.5 reshape.59
  10.5 1.1 %fusion.21 = f32[32,64,64]{1,2,0:T(8,128)S(1)} fusion(bf16[32,64,64]{2,1,0:T(8,128)(2,1)S(1)} %reshape.59, f32[3,64,64]{2,1,0:T(8,128)S(1)} %copy-done.1), kind=kOutput, calls=%fused_computation.34 | convolution fusion | flops 50331648 | bytes 1081344 | tf_op jit(solution)/shard_map/qab,bj->qaj/dot_general | solution.py:18
  11.7 0.7 multiply_reduce_fusion.2
  12.4 0.6 convolution_bitcast_fusion.4
  13.0 1.0 convolution_convert_fusion.2
  14.0 0.5 convert_element_type.61
  14.4 0.5 reshape.61
  15.0 1.1 %fusion.11 = f32[32,64,64]{1,2,0:T(8,128)S(1)} fusion(bf16[32,64,64]{2,1,0:T(8,128)(2,1)S(1)} %reshape.61, f32[3,64,64]{2,1,0:T(8,128)S(1)} %copy-done.1), kind=kOutput, calls=%fused_computation.24 | convolution fusion | flops 50331648 | bytes 1081344 | tf_op jit(solution)/shard_map/qab,bj->qaj/dot_general | solution.py:18
  16.1 0.7 multiply_reduce_fusion
  16.8 0.6 convolution_bitcast_fusion
  17.4 1.0 convolution_convert_fusion
  18.4 0.5 convert_element_type.65
  18.9 0.1 copy.27
  19.0 0.1 fusion.4.blk
  19.1 82.8 %shard_map.64 = f32[1024,256]{1,0:T(8,128)} custom-call(bf16[32,12416]{1,0:T(8,128)(2,1)S(1)} %fusion.4.blk, bf16[1024,12288]{1,0:T(8,128)(2,1)} %docs.1, f32[1024,1]{1,0:T(8,128)S(1)} %copy.28.factor), custom_call_target="tpu_custom_call" | custom-call | flops 6442450944 | bytes 25165824 | tf_op jit(solution)/shard_map/pallas_call | solution.py:224
  101.8 2.3 %copy.36 = f32[1024,256]{1,0:T(8,128)} copy(f32[1024,256]{1,0:T(8,128)} %shard_map.64) | data formatting | bytes 2097152
  (3 shorter events, 0.0 us)
Async XLA Ops:
  0.0 5.5 %copy-start = (bf16[32,12288]{1,0:T(8,128)(2,1)S(1)}, bf16[32,12288]{1,0:T(8,128)(2,1)}, u32[]{:S(2)}) copy-start(bf16[32,12288]{1,0:T(8,128)(2,1)} %param.7) | copy-start | bytes 2359300
  5.0 1.1 %copy-start.1 = (f32[3,64,64]{2,1,0:T(8,128)S(1)}, f32[3,64,64]{2,1,0:T(8,128)}, u32[]{:S(2)}) copy-start(f32[3,64,64]{2,1,0:T(8,128)} %param.9) | copy-start | bytes 147460
  5.5 1.7 %copy-start.2 = (f32[3,64,64]{2,1,0:T(8,128)S(1)}, f32[3,64,64]{2,1,0:T(8,128)}, u32[]{:S(2)}) copy-start(f32[3,64,64]{2,1,0:T(8,128)} %param.8) | copy-start | bytes 147460

commit v5 on v3

--- a/solution.py
+++ b/solution.py
@@ -26,7 +26,7 @@
 
 
 def kernel(
-    n, pair, tiles, blk, docs, factor, out, got, docs_v, acc, mine, theirs, selfs,
+    n, pair, tiles, blk, docs, out, self_out, got, docs_v, acc, mine, theirs, selfs,
     their_selfs, send_sem, recv_sem, doc_sem, ex_send, ex_recv,
 ):
     me = lax.axis_index("docs")
@@ -196,27 +196,29 @@
         mine[pl.ds(t * tile, tile), :] = product(last, t).astype(bf16)
         swap(t).start()
     swap(tiles).wait()
-    scale = lax.rsqrt(selfs[0:1, :] + their_selfs[0:1, :])
+    self_out[...] = selfs[...] + their_selfs[...]
     for t in range(tiles):
         rows = pl.ds(t * tile, tile)
         swap(t).wait()
-        total = mine[rows, :].astype(f32) + theirs[rows, :].astype(f32)
-        out[rows, :] = total * scale * factor[rows, :]
+        out[rows, :] = mine[rows, :].astype(f32) + theirs[rows, :].astype(f32)
     for c in range(chunks):
         own_each(c, False)
         line_each(c, False)
 
 
-def gather_and_score(n, pair, block, docs, factor):
+def gather_and_score(n, pair, block, docs):
     q, wide = block.shape
     rows, features = docs.shape
     queries, tiles = n * q, 4
     vmem = pl.BlockSpec(memory_space=pltpu.VMEM)
     return pl.pallas_call(
         functools.partial(kernel, n, pair, tiles),
-        out_shape=jax.ShapeDtypeStruct((rows, queries), f32),
-        in_specs=[vmem, pl.BlockSpec(memory_space=pl.ANY), vmem],
-        out_specs=vmem,
+        out_shape=(
+            jax.ShapeDtypeStruct((rows, queries), f32),
+            jax.ShapeDtypeStruct((16, queries), f32),
+        ),
+        in_specs=[vmem, pl.BlockSpec(memory_space=pl.ANY)],
+        out_specs=(vmem, vmem),
         scratch_shapes=[
             pltpu.VMEM((queries, wide), bf16),
             pltpu.VMEM((rows, features), bf16),
@@ -239,7 +241,7 @@
             bytes_accessed=2 * rows * features,
             transcendentals=0,
         ),
-    )(block, docs, factor)
+    )(block, docs)
 
 
 def shards(n, pair, doc_grads, query_grads, basis_in, basis_out, eigen, token_counts):
@@ -259,8 +261,9 @@
     lower = (self_part - upper.astype(f32)).astype(bf16)
     blocks.append(jnp.pad(jnp.stack([upper, lower], axis=1), ((0, 0), (0, 126))))
     block = jnp.concatenate(blocks, axis=1)
-    factor = (ref_tokens / token_counts.astype(f32))[:, None]
-    return gather_and_score(n, pair, block, doc_grads, factor)
+    totals, self_terms = gather_and_score(n, pair, block, doc_grads)
+    factor = ref_tokens / token_counts.astype(f32)
+    return totals * lax.rsqrt(self_terms[0])[None, :] * factor[:, None]
 
 
 def solution(mesh):

time: 103 us -> 104 us (level)
  matrix products: 10.2 us -> 12.1 us
  local copies, waits for them, and re-layouts: 5.89 us -> 4.52 us
  other arithmetic: 3.14 us -> 4.27 us
  Pallas kernels: 81.4 us -> 80.3 us
    dot_general x3, matrix products: 1.74 us -> 4.89 us  [precondition(): mapped = jnp.einsum('qij,ai->qaj', scaled, basis_in, precision=high)]
    unnamed x7 -> x4, local copies, waits for them, and re-layouts: 2.28 us -> 0.01 us
    dot_general x3, matrix products: 2.98 us -> 1.73 us  [precondition(): mapped = jnp.einsum('qaj,bj->qab', mapped, basis_out, precision=high)]
    mul x0 -> x1, other arithmetic: none -> 1.17 us  [shards(): return totals * lax.rsqrt(self_terms[0])[None, :] * factor[:, None]]
    slice x1, local copies, waits for them, and re-layouts: 0.05 us -> 1.18 us  [shards(): gradient = query_grads[:, m * size:(m + 1) * size]]
    pallas_call x1, Pallas kernels: 81.4 us -> 80.3 us  [gather_and_score(): pl.pallas_call(functools.partial(kernel, n, pair, tiles), out_shape=(jax....]
where the time goes in v5:
time: 104 us; the launch traced here: 103 us
  Pallas kernels  80.3 us (77%)
  matrix products  12.1 us (12%)
  local copies, waits for them, and re-layouts  4.52 us (4%)
  other arithmetic  4.27 us (4%)
  between operations  2.02 us (2%)
    pallas_call x1, Pallas kernels, gather_and_score(): pl.pallas_call(functools.partial(kernel, n, pair, tiles), out_shape=(jax....  80.3 us
    dot_general x3, matrix products, precondition(): mapped = jnp.einsum('qij,ai->qaj', scaled, basis_in, precision=high)  4.89 us
    dot_general x3, matrix products, precondition(): rotated = jnp.einsum('qab,bj->qaj', gradient, basis_out, precision=high)  3.41 us
    dot_general x3, matrix products, precondition(): rotated = jnp.einsum('qaj,ai->qij', rotated, basis_in, precision=high)  2.11 us

profile of v5, /device:TPU:0, one launch (start us, length us, event | category | flops | bytes accessed | tf_op | source)
XLA Modules:
  0.0 103.3 jit_solution(8103601316101574232)
XLA Ops:
  0.0 0.0 copy-start
  0.0 1.5 %slice_reduce_fusion.1 = (f32[]{:T(128)}, f32[]{:T(128)}, f32[]{:T(128)}) fusion(f32[3,64,64]{2,1,0:T(8,128)} %param.10), kind=kLoop, calls=%fused_computation.45 | loop fusion | flops 12285 | bytes 49164 | tf_op jit(solution)/shard_map/reduce_sum | solution.py:20
  3.4 0.7 convert_divide_fusion
  4.1 0.8 add_bitcast_fusion.1
  4.9 0.1 copy.13
  5.0 0.1 copy.14
  5.1 0.1 copy.12
  5.2 1.2 %fusion.36 = (bf16[32,4096]{1,0:T(8,128)(2,1)S(1)}, bf16[32,4096]{1,0:T(8,128)(2,1)S(1)}, bf16[32,4096]{1,0:T(8,128)(2,1)S(1)}) fusion(bf16[32,12288]{1,0:T(8,128)(2,1)} %param.7), kind=kLoop, calls=%fused_computation.62 | loop fusion | bytes 1572864 | tf_op jit(solution)/shard_map/slice | solution.py:255
  6.3 0.0 copy-start.1
  6.3 0.5 reshape.61
  6.9 0.0 copy-done
  6.9 1.1 %fusion.16 = f32[32,64,64]{1,2,0:T(8,128)S(1)} fusion(bf16[32,64,64]{2,1,0:T(8,128)(2,1)S(1)} %reshape.61, f32[3,64,64]{2,1,0:T(8,128)S(1)} %copy-done), kind=kOutput, calls=%fused_computation.30 | convolution fusion | flops 50331648 | bytes 1081344 | tf_op jit(solution)/shard_map/qab,bj->qaj/dot_general | solution.py:18
  8.0 0.0 copy-done.1
  8.0 0.7 multiply_reduce_fusion.1
  8.7 1.6 %convolution_bitcast_fusion.2 = f32[32,64,64]{2,1,0:T(8,128)S(1)} fusion(f32[32,64,64]{1,2,0:T(8,128)S(1)} %get-tuple-element.23, f32[64,64]{0,1:T(8,128)S(1)} %copy.13, f32[3,64,64]{2,1,0:T(8,128)S(1)} %copy-done.1), kind=kOutput, calls=%fused_computation.4 | convolution fusion | flops 50462720 | bytes 1638400 | tf_op jit(solution)/shard_map/qij,ai->qaj/dot_general | solution.py:23
  10.4 0.6 convolution_convert_fusion.1
  11.0 0.5 convert_element_type.63
  11.4 0.5 reshape.60
  12.0 1.1 %fusion.21 = f32[32,64,64]{1,2,0:T(8,128)S(1)} fusion(bf16[32,64,64]{2,1,0:T(8,128)(2,1)S(1)} %reshape.60, f32[3,64,64]{2,1,0:T(8,128)S(1)} %copy-done), kind=kOutput, calls=%fused_computation.35 | convolution fusion | flops 50331648 | bytes 1081344 | tf_op jit(solution)/shard_map/qab,bj->qaj/dot_general | solution.py:18
  13.1 0.7 multiply_reduce_fusion.2
  13.8 1.6 %convolution_bitcast_fusion.4 = f32[32,64,64]{2,1,0:T(8,128)S(1)} fusion(f32[32,64,64]{1,2,0:T(8,128)S(1)} %get-tuple-element.21, f32[64,64]{0,1:T(8,128)S(1)} %copy.12, f32[3,64,64]{2,1,0:T(8,128)S(1)} %copy-done.1), kind=kOutput, calls=%fused_computation.6 | convolution fusion | flops 50462720 | bytes 1638400 | tf_op jit(solution)/shard_map/qij,ai->qaj/dot_general | solution.py:23
  15.4 0.6 convolution_convert_fusion.2
  16.0 0.5 convert_element_type.61
  16.5 0.5 reshape.62
  17.0 1.1 %fusion.11 = f32[32,64,64]{1,2,0:T(8,128)S(1)} fusion(bf16[32,64,64]{2,1,0:T(8,128)(2,1)S(1)} %reshape.62, f32[3,64,64]{2,1,0:T(8,128)S(1)} %copy-done), kind=kOutput, calls=%fused_computation.25 | convolution fusion | flops 50331648 | bytes 1081344 | tf_op jit(solution)/shard_map/qab,bj->qaj/dot_general | solution.py:18
  18.2 0.7 multiply_reduce_fusion
  18.9 1.6 %convolution_bitcast_fusion = f32[32,64,64]{2,1,0:T(8,128)S(1)} fusion(f32[32,64,64]{1,2,0:T(8,128)S(1)} %get-tuple-element.19, f32[64,64]{0,1:T(8,128)S(1)} %copy.14, f32[3,64,64]{2,1,0:T(8,128)S(1)} %copy-done.1), kind=kOutput, calls=%fused_computation.2 | convolution fusion | flops 50462720 | bytes 1638400 | tf_op jit(solution)/shard_map/qij,ai->qaj/dot_general | solution.py:23
  20.5 0.6 convolution_convert_fusion
  21.1 0.5 convert_element_type.65
  21.6 0.1 copy.15
  21.7 0.1 fusion.4.blk
  21.8 80.3 %shard_map.64 = (f32[1024,256]{1,0:T(8,128)S(1)}, f32[16,256]{1,0:T(8,128)S(1)}) custom-call(bf16[32,12416]{1,0:T(8,128)(2,1)S(1)} %fusion.4.blk, bf16[1024,12288]{1,0:T(8,128)(2,1)} %docs.1), custom_call_target="tpu_custom_call" | custom-call | flops 6442450944 | bytes 25165824 | tf_op jit(solution)/shard_map/pallas_call | solution.py:214
  102.1 1.2 %multiply_multiply_fusion = f32[1024,256]{1,0:T(8,128)} fusion(f32[1024,256]{1,0:T(8,128)S(1)} %get-tuple-element.7, f32[1024]{0:T(1024)S(1)} %convert_divide_fusion, f32[256]{0:T(256)S(1)} %bitcast.77), kind=kLoop, calls=%fused_computation.11 | loop fusion | flops 524288 | bytes 2102272 | tf_op jit(solution)/shard_map/mul | solution.py:266
  (4 shorter events, 0.0 us)
Async XLA Ops:
  0.0 6.9 %copy-start = (f32[3,64,64]{2,1,0:T(8,128)S(1)}, f32[3,64,64]{2,1,0:T(8,128)}, u32[]{:S(2)}) copy-start(f32[3,64,64]{2,1,0:T(8,128)} %param.9) | copy-start | bytes 147460
  6.3 1.7 %copy-start.1 = (f32[3,64,64]{2,1,0:T(8,128)S(1)}, f32[3,64,64]{2,1,0:T(8,128)}, u32[]{:S(2)}) copy-start(f32[3,64,64]{2,1,0:T(8,128)} %param.8) | copy-start | bytes 147460

commit v6 on v3

--- a/solution.py
+++ b/solution.py
@@ -40,8 +40,8 @@
     q = blk.shape[0]
     wide = blk.shape[1]
     features = docs.shape[1]
-    third = features // 3
-    edges = (0, third, 2 * third, 2 * third + third // 4 * 3, features)
+    fine = features // 96
+    edges = tuple(fine * step for step in (0, 24, 48, 72, 88, 96))
     chunks = len(edges) - 1
     tile = docs.shape[0] // tiles
 
@@ -225,9 +225,9 @@
             pltpu.VMEM((rows, queries), bf16),
             pltpu.VMEM((16, queries), f32),
             pltpu.VMEM((16, queries), f32),
-            pltpu.SemaphoreType.DMA((3, n, 8)),
-            pltpu.SemaphoreType.DMA((n, 8)),
-            pltpu.SemaphoreType.DMA((4,)),
+            pltpu.SemaphoreType.DMA((3, n, 10)),
+            pltpu.SemaphoreType.DMA((n, 10)),
+            pltpu.SemaphoreType.DMA((5,)),
             pltpu.SemaphoreType.DMA((tiles + 1,)),
             pltpu.SemaphoreType.DMA((tiles + 1,)),
         ],

time: 103 us -> 104 us (level)
  no operation moved by 1% of the time
where the time goes in v6:
time: 104 us; the launch traced here: 103 us
  Pallas kernels  82 us (79%)
  matrix products  10.2 us (10%)
  local copies, waits for them, and re-layouts  5.89 us (6%)
  other arithmetic  3.14 us (3%)
  between operations  2.06 us (2%)
    pallas_call x1, Pallas kernels, gather_and_score(): pl.pallas_call(functools.partial(kernel, n, pair, tiles), out_shape=jax.S...  82 us
    dot_general x3, matrix products, precondition(): rotated = jnp.einsum('qab,bj->qaj', gradient, basis_out, precision=high)  3.42 us
    dot_general x3, matrix products, precondition(): mapped = jnp.einsum('qaj,bj->qab', mapped, basis_out, precision=high)  2.98 us
    unnamed x7, local copies, waits for them, and re-layouts  2.28 us
    dot_general x3, matrix products, precondition(): rotated = jnp.einsum('qaj,ai->qij', rotated, basis_in, precision=high)  2.1 us

profile of v6, /device:TPU:0, one launch (start us, length us, event | category | flops | bytes accessed | tf_op | source)
XLA Modules:
  0.0 103.3 jit_solution(4562665838119692038)
XLA Ops:
  0.0 0.0 copy-start
  0.0 1.6 %slice_reduce_fusion.1 = (f32[]{:T(128)}, f32[]{:T(128)}, f32[]{:T(128)}) fusion(f32[3,64,64]{2,1,0:T(8,128)} %param.10), kind=kLoop, calls=%fused_computation.44 | loop fusion | flops 12285 | bytes 49164 | tf_op jit(solution)/shard_map/reduce_sum | solution.py:20
  3.5 0.7 convert_divide_fusion
  4.2 0.8 add_bitcast_fusion.1
  5.0 0.0 copy-start.1
  5.0 0.1 copy.22
  5.0 0.1 copy.25
  5.1 0.1 copy.19
  5.2 0.2 copy.28.factor
  5.5 0.0 copy-done
  5.5 0.1 fusion.36
  5.5 0.0 copy-start.2
  5.5 0.5 reshape.60
  6.1 0.0 copy-done.1
  6.1 1.1 %fusion.16 = f32[32,64,64]{1,2,0:T(8,128)S(1)} fusion(bf16[32,64,64]{2,1,0:T(8,128)(2,1)S(1)} %reshape.60, f32[3,64,64]{2,1,0:T(8,128)S(1)} %copy-done.1), kind=kOutput, calls=%fused_computation.29 | convolution fusion | flops 50331648 | bytes 1081344 | tf_op jit(solution)/shard_map/qab,bj->qaj/dot_general | solution.py:18
  7.2 0.0 copy-done.2
  7.2 0.7 multiply_reduce_fusion.1
  7.9 0.6 convolution_bitcast_fusion.2
  8.5 1.0 convolution_convert_fusion.1
  9.5 0.5 convert_element_type.63
  10.0 0.5 reshape.59
  10.5 1.1 %fusion.21 = f32[32,64,64]{1,2,0:T(8,128)S(1)} fusion(bf16[32,64,64]{2,1,0:T(8,128)(2,1)S(1)} %reshape.59, f32[3,64,64]{2,1,0:T(8,128)S(1)} %copy-done.1), kind=kOutput, calls=%fused_computation.34 | convolution fusion | flops 50331648 | bytes 1081344 | tf_op jit(solution)/shard_map/qab,bj->qaj/dot_general | solution.py:18
  11.7 0.7 multiply_reduce_fusion.2
  12.4 0.6 convolution_bitcast_fusion.4
  13.0 1.0 convolution_convert_fusion.2
  14.0 0.5 convert_element_type.61
  14.4 0.5 reshape.61
  15.0 1.1 %fusion.11 = f32[32,64,64]{1,2,0:T(8,128)S(1)} fusion(bf16[32,64,64]{2,1,0:T(8,128)(2,1)S(1)} %reshape.61, f32[3,64,64]{2,1,0:T(8,128)S(1)} %copy-done.1), kind=kOutput, calls=%fused_computation.24 | convolution fusion | flops 50331648 | bytes 1081344 | tf_op jit(solution)/shard_map/qab,bj->qaj/dot_general | solution.py:18
  16.1 0.7 multiply_reduce_fusion
  16.8 0.6 convolution_bitcast_fusion
  17.4 1.0 convolution_convert_fusion
  18.4 0.5 convert_element_type.65
  18.9 0.1 copy.27
  19.0 0.1 fusion.4.blk
  19.1 82.0 %shard_map.64 = f32[1024,256]{1,0:T(8,128)} custom-call(bf16[32,12416]{1,0:T(8,128)(2,1)S(1)} %fusion.4.blk, bf16[1024,12288]{1,0:T(8,128)(2,1)} %docs.1, f32[1024,1]{1,0:T(8,128)S(1)} %copy.28.factor), custom_call_target="tpu_custom_call" | custom-call | flops 6442450944 | bytes 25165824 | tf_op jit(solution)/shard_map/pallas_call | solution.py:215
  101.0 2.3 %copy.36 = f32[1024,256]{1,0:T(8,128)} copy(f32[1024,256]{1,0:T(8,128)} %shard_map.64) | data formatting | bytes 2097152
  (3 shorter events, 0.0 us)
Async XLA Ops:
  0.0 5.5 %copy-start = (bf16[32,12288]{1,0:T(8,128)(2,1)S(1)}, bf16[32,12288]{1,0:T(8,128)(2,1)}, u32[]{:S(2)}) copy-start(bf16[32,12288]{1,0:T(8,128)(2,1)} %param.7) | copy-start | bytes 2359300
  5.0 1.1 %copy-start.1 = (f32[3,64,64]{2,1,0:T(8,128)S(1)}, f32[3,64,64]{2,1,0:T(8,128)}, u32[]{:S(2)}) copy-start(f32[3,64,64]{2,1,0:T(8,128)} %param.9) | copy-start | bytes 147460
  5.5 1.7 %copy-start.2 = (f32[3,64,64]{2,1,0:T(8,128)S(1)}, f32[3,64,64]{2,1,0:T(8,128)}, u32[]{:S(2)}) copy-start(f32[3,64,64]{2,1,0:T(8,128)} %param.8) | copy-start | bytes 147460
